TPU v7x, 512 devices: a whole 4x8x8 slice. The times are simulated.
512 devices in a mesh: state: 32 (over x, z), obs: 16 (over y, core).
Axes of the slice: x: 4, y: 8, z: 8, core: 2. Of those that a mesh axis runs over, the one named last changes fastest.
Arguments:
- state_mean: float32 [1024, 1024], P(('state', 'obs')), may hold values from -6 to 6
- state_anom: bfloat16 [1024, 80, 1024], P(('state', 'obs')), may hold values from -6 to 6
- obs_prior: bfloat16 [2, 80, 16384], P(None, None, ('state', 'obs')), may hold values from -6 to 6
- obs_value: bfloat16 [2, 16384], P(None, ('state', 'obs')), may hold values from -8 to 8
- obs_var: bfloat16 [2, 16384], P(None, ('state', 'obs')), may hold values from 0.29882812 to 3
- obs_weight: float32 [8, 16384], P(None, 'state'), may hold values from 0.1 to 0.5
- obs_home: int32 [16384], P('state'), may hold values from 0 to 131071, as said below
- tile_obs: int32 [2, 1024, 256], P(None, ('state', 'obs')), may hold values from 0 to 16383, as said below
- taper: bfloat16 [2, 1024, 256, 128], P(None, ('state', 'obs')), may hold values from 0.19921875 to 1
Outputs:
- analysis_mean: float32 [1024, 1024], P(('state', 'obs'))
- analysis_anom: bfloat16 [1024, 80, 1024], P(('state', 'obs'))
Inputs may be any that keep to these rules, and one draw needn't show every extreme that they name: `tile_obs`: each tile's 256 entries of one colour are distinct observations, all owned by devices whose index along state differs from the tile's by at most one; observation numbers run owner by owner, 512 for each index of state. `obs_home`: each observation's column lies in a tile held by some device with the same index along state as the observation's owner.
All inputs are finite; a program needn't handle non-finite values.
Results may differ from a plain program's by a relative error of at most 0.009.
Values may be sent and summed in bfloat16 or wider, within the bound.
No kernel may reach another device: no remote copies, remote signals or barrier semaphores. Data moves between devices by JAX's collectives and lax.ppermute only.
A program may use at most 64 MiB of HBM per device.

v0:
```python
import jax
import jax.numpy as jnp
from jax import lax
from jax.sharding import PartitionSpec as P


def extended(block, sides, width):
    for axis, dim in sides:
        count = lax.axis_size(axis)
        forward = [(i, i + 1) for i in range(count - 1)]
        backward = [(target, source) for source, target in forward]
        low = lax.ppermute(
            lax.slice_in_dim(block, block.shape[dim] - width, None, axis=dim), axis, forward
        )
        high = lax.ppermute(lax.slice_in_dim(block, 0, width, axis=dim), axis, backward)
        block = jnp.concatenate([low, block, high], axis=dim)
    return block


def obs_package(records):
    member_count = records.shape[0] - 2
    ensemble = records[:member_count].astype(jnp.float32)
    observed = records[member_count].astype(jnp.float32)
    error_var = records[member_count + 1].astype(jnp.float32)
    centre = jnp.mean(ensemble, axis=0)
    anomaly = ensemble - centre
    spread = jnp.sum(anomaly * anomaly, axis=0) / (member_count - 1)
    kalman_gain = 1.0 / (spread + error_var)
    sqrt_factor = 1.0 / (1.0 + jnp.sqrt(error_var * kalman_gain))
    coef_anom = sqrt_factor * kalman_gain / (member_count - 1)
    coef_mean = kalman_gain * (observed - centre) / (member_count - 1)
    return (anomaly, coef_anom, coef_mean)


def update_block(current_mean, current_anom, anomaly_rows, coef_anom, coef_mean, colour_taper):
    tile_count, list_len, tile_width = colour_taper.shape
    levels = current_anom.shape[2] // tile_width
    basis_rows = anomaly_rows.astype(jnp.bfloat16).reshape(tile_count, list_len, -1)
    projection = jnp.einsum(
        "tjm,tmc->tjc", basis_rows, current_anom, preferred_element_type=jnp.float32
    )
    proj_levels = projection.reshape(tile_count, list_len, levels, tile_width)
    taper_levels = colour_taper.astype(jnp.float32)[:, :, None, :]
    mean_coef = coef_mean.reshape(tile_count, list_len, 1, 1)
    anom_coef = coef_anom.reshape(tile_count, list_len, 1, 1)
    new_mean = current_mean + jnp.sum(taper_levels * mean_coef * proj_levels, axis=1).reshape(
        tile_count, -1
    )
    scaled = (
        (taper_levels * anom_coef * proj_levels)
        .astype(jnp.bfloat16)
        .reshape(tile_count, list_len, -1)
    )
    shift_term = jnp.einsum("tjm,tjc->tmc", basis_rows, scaled, preferred_element_type=jnp.float32)
    new_anom = (current_anom.astype(jnp.float32) - shift_term).astype(jnp.bfloat16)
    return (new_mean, new_anom)


def local(
    state_mean, state_anom, obs_prior, obs_value, obs_var, obs_weight, obs_home, tile_obs, taper
):
    tile_count, members, cell_count = state_anom.shape
    tile_width = taper.shape[3]
    levels = cell_count // tile_width
    obs_groups = lax.axis_size("obs")
    region_size = obs_groups * obs_prior.shape[2]
    state_row = lax.axis_index("state")
    current_mean = state_mean
    current_anom = state_anom
    ensemble_now = obs_prior[0]
    for colour in range(obs_prior.shape[0]):
        records = jnp.concatenate([ensemble_now, obs_value[colour][None], obs_var[colour][None]], 0)
        obs_ids = tile_obs[colour].reshape(-1)
        region_off = obs_ids // region_size - state_row + 1
        region_slot = obs_ids % region_size
        anomaly, coef_anom, coef_mean = obs_package(records)
        package = jnp.concatenate([anomaly, coef_anom[None], coef_mean[None]], 0)
        gathered = lax.all_gather(package[None], "obs", axis=2, tiled=True)
        beside_all = extended(gathered, (("state", 0),), 1)
        picked = beside_all[region_off, :, region_slot]
        anomaly_rows = picked[:, :members]
        coef_anom = picked[:, members]
        coef_mean = picked[:, members + 1]
        new_mean, new_anom = update_block(
            current_mean, current_anom, anomaly_rows, coef_anom, coef_mean, taper[colour]
        )
        if colour == 0:
            first_tile = (state_row * obs_groups + lax.axis_index("obs")) * tile_count
            home_tile = obs_home // tile_width - first_tile
            inside = ((home_tile >= 0) & (home_tile < tile_count)).astype(jnp.float32)
            local_tile = jnp.clip(home_tile, 0, tile_count - 1)
            home_col = obs_home % tile_width
            mean_change = (new_mean - current_mean).reshape(tile_count, levels, tile_width)[
                local_tile, :, home_col
            ]
            before = current_anom.reshape(tile_count, members, levels, tile_width)[
                local_tile, :, :, home_col
            ].astype(jnp.float32)
            updated = new_anom.reshape(tile_count, members, levels, tile_width)[
                local_tile, :, :, home_col
            ].astype(jnp.float32)
            change = updated - before + mean_change[:, None, :]
            increment_term = (
                jnp.einsum("jml,lj->mj", change, obs_weight, precision=lax.Precision.HIGHEST)
                * inside[None, :]
            )
            increment = lax.psum_scatter(increment_term, "obs", scatter_dimension=1, tiled=True)
            ensemble_now = (obs_prior[1].astype(jnp.float32) + increment).astype(jnp.bfloat16)
        current_mean = new_mean
        current_anom = new_anom
    return (current_mean, current_anom)


def solution(mesh):
    in_specs = (
        P(("state", "obs"), None),
        P(("state", "obs"), None, None),
        P(None, None, ("state", "obs")),
        P(None, ("state", "obs")),
        P(None, ("state", "obs")),
        P(None, "state"),
        P("state"),
        P(None, ("state", "obs"), None),
        P(None, ("state", "obs"), None, None),
    )
    out_specs = (P(("state", "obs"), None), P(("state", "obs"), None, None))
    return jax.shard_map(local, mesh=mesh, in_specs=in_specs, out_specs=out_specs, check_vma=False)
```

profile of v0, /device:TPU:1, one launch (start us, length us, event | category | flops | bytes accessed | tf_op | source)
XLA Modules:
  0.0 181.6 jit_solution(9451828262632047815)
XLA Ops:
  10.5 21.6 %all-gather = f32[82,512]{0,1:T(8,128)S(1)} all-gather(f32[82,32]{0,1:T(8,128)S(1)} %pad_maximum_fusion.2), channel_id=2, replica_groups=mesh['state'=32,'obs'=16] {'obs'}, dimensions={1}, use_global_device_ids=true | all-gather | bytes 178432 | tf_op jit(solution)/shard_map/all_gather | solution.py:78
  32.1 2.1 %collective-permute-start = (f32[1,82,512]{1,2,0:T(8,128)S(1)}, f32[1,82,512]{1,2,0:T(8,128)S(1)}, u32[]{:S(2)}, u32[]{:S(2)}) collective-permute-start(f32[1,82,512]{1,2,0:T(8,128)S(1)} %bitcast.97), channel_id=1, source_target_pairs={{0,16},{16,32},{32,48},{48,64},{64,80},{80,96},{96,112},{112,128},... | collective-permute-start | bytes 503816 | tf_op jit(solution)/shard_map/ppermute | solution.py:12
  39.0 1.6 copy.72
  40.5 2.3 %gather_fusion.2 = bf16[512,80,8]{1,2,0:T(8,128)(2,1)S(1)} fusion(bf16[2,80,8,128]{1,2,3,0:T(8,128)(2,1)S(1)} %copy.65, s32[512]{0:T(512)S(1)} %fusion.13), kind=kCustom, calls=%fused_computation.2 | custom fusion | bytes 1314816 | tf_op jit(solution)/shard_map/gather | solution.py:96
  42.9 1.5 collective-permute-done.1
  44.5 3.7 %gather_fusion = f32[512,82]{1,0:T(8,128)S(1)} fusion(f32[3,82,512]{1,2,0:T(8,128)S(1)} %pad_maximum_fusion, s32[512]{0:T(512)S(1)} %bitcast.88), kind=kCustom, calls=%fused_computation | custom fusion | bytes 339968 | tf_op jit(solution)/shard_map/gather | solution.py:80
  49.4 1.5 mul.158
  50.9 1.7 mul.159
  52.6 1.5 mul.164
  54.1 2.7 %mul.165 = f32[2,256,1024]{2,1,0:T(8,128)} reshape(f32[2,256,8,128]{3,2,1,0:T(8,128)} %mul.164) | data formatting | bytes 4194304 | tf_op jit(solution)/shard_map/mul | solution.py:50
  56.9 1.5 multiply_reduce_fusion.1
  59.3 2.3 %gather_fusion.1 = bf16[512,80,8]{1,2,0:T(8,128)(2,1)S(1)} fusion(bf16[2,80,8,128]{1,2,3,0:T(8,128)(2,1)S(1)} %copy.64, s32[512]{0:T(512)S(1)} %fusion.13), kind=kCustom, calls=%fused_computation.1 | custom fusion | bytes 1314816 | tf_op jit(solution)/shard_map/gather | solution.py:99
  61.8 3.7 %gather_fusion.3 = f32[512,8]{1,0:T(8,128)S(1)} fusion(f32[2,8,128]{1,2,0:T(8,128)S(1)} %copy.66, s32[512]{0:T(512)S(1)} %fusion.13), kind=kCustom, calls=%fused_computation.3 | custom fusion | bytes 36864 | tf_op jit(solution)/shard_map/gather | solution.py:93
  65.5 3.8 %fusion = f32[512,1,80]{2,1,0:T(1,128)S(1)} fusion(f32[8,512,1]{0,2,1:T(1,128)S(1)} %copy-done.6, bf16[512,80,8]{1,2,0:T(8,128)(2,1)S(1)} %gather_fusion.2, bf16[512,80,8]{1,2,0:T(8,128)(2,1)S(1)} %gather_fusion.1, f32[512,8]{1,0:T(8,128)S(1)} %gather_fusion.3), kind=kOutput, calls=%fused_computation.7 | convolution fusion | flops 5242880 | bytes 1507328 | tf_op jit(solution)/shard_map/jml,lj->mj/dot_general | solution.py:104
  70.2 58.3 %reduce-scatter.2.cloned.1.call-done = f32[80,32]{0,1:T(8,128)} async-done(((f32[80,512]{0,1:T(8,128)}), f32[80,32]{0,1:T(8,128)}) %reduce-scatter.2.cloned.1.call-update) | async-done | bytes 10256 | tf_op jit(solution)/shard_map/reduce_scatter | solution.py:107
  129.8 17.1 %all-gather.1 = f32[82,512]{0,1:T(8,128)S(1)} all-gather(f32[82,32]{0,1:T(8,128)S(1)} %pad_maximum_fusion.3), channel_id=3, replica_groups=mesh['state'=32,'obs'=16] {'obs'}, dimensions={1}, use_global_device_ids=true | all-gather | bytes 178432 | tf_op jit(solution)/shard_map/all_gather | solution.py:78
  146.9 3.4 %collective-permute-start.2 = (f32[1,82,512]{1,2,0:T(8,128)S(1)}, f32[1,82,512]{1,2,0:T(8,128)S(1)}, u32[]{:S(2)}, u32[]{:S(2)}) collective-permute-start(f32[1,82,512]{1,2,0:T(8,128)S(1)} %bitcast.100), channel_id=1, source_target_pairs={{0,16},{16,32},{32,48},{48,64},{64,80},{80,96},{96,112},{112,128},... | collective-permute-start | bytes 503816 | tf_op jit(solution)/shard_map/ppermute | solution.py:12
  151.8 4.0 %collective-permute-done.2 = f32[1,82,512]{1,2,0:T(8,128)S(1)} collective-permute-done((f32[1,82,512]{1,2,0:T(8,128)S(1)}, f32[1,82,512]{1,2,0:T(8,128)S(1)}, u32[]{:S(2)}, u32[]{:S(2)}) %collective-permute-start.2) | collective-permute-done | bytes 167968 | tf_op jit(solution)/shard_map/ppermute | solution.py:12
  155.8 3.8 %collective-permute-done.3 = f32[1,82,512]{1,2,0:T(8,128)S(1)} collective-permute-done((f32[1,82,512]{1,2,0:T(8,128)S(1)}, f32[1,82,512]{1,2,0:T(8,128)S(1)}, u32[]{:S(2)}, u32[]{:S(2)}) %collective-permute-start.3) | collective-permute-done | bytes 167968 | tf_op jit(solution)/shard_map/ppermute | solution.py:15
  159.7 3.7 %gather_fusion.4 = f32[512,82]{1,0:T(8,128)S(1)} fusion(f32[3,82,512]{1,2,0:T(8,128)S(1)} %pad_maximum_fusion.1, s32[512]{0:T(512)S(1)} %bitcast.87), kind=kCustom, calls=%fused_computation.4 | custom fusion | bytes 339968 | tf_op jit(solution)/shard_map/gather | solution.py:80
  164.0 1.5 mul.179
  165.5 1.7 mul.180
  167.2 1.5 mul.185
  168.7 2.7 %mul.186 = f32[2,256,1024]{2,1,0:T(8,128)} reshape(f32[2,256,8,128]{3,2,1,0:T(8,128)} %mul.185) | data formatting | bytes 4194304 | tf_op jit(solution)/shard_map/mul | solution.py:50
  (74 shorter events, 18.2 us)
Async XLA Ops:
  7.2 121.3 %reduce-scatter.2.cloned.1.call-start = ((), (), s32[]{:S(2)}) async-start(), calls=%async_computation.1 | async-start | bytes 278528 | tf_op jit(solution)/shard_map/reduce_scatter | solution.py:107
  32.1 10.8 %collective-permute-start = (f32[1,82,512]{1,2,0:T(8,128)S(1)}, f32[1,82,512]{1,2,0:T(8,128)S(1)}, u32[]{:S(2)}, u32[]{:S(2)}) collective-permute-start(f32[1,82,512]{1,2,0:T(8,128)S(1)} %bitcast.97), channel_id=1, source_target_pairs={{0,16},{16,32},{32,48},{48,64},{64,80},{80,96},{96,112},{112,128},... | collective-permute-start | bytes 503816 | tf_op jit(solution)/shard_map/ppermute | solution.py:12
  34.1 10.3 %collective-permute-start.1 = (f32[1,82,512]{1,2,0:T(8,128)S(1)}, f32[1,82,512]{1,2,0:T(8,128)S(1)}, u32[]{:S(2)}, u32[]{:S(2)}) collective-permute-start(f32[1,82,512]{1,2,0:T(8,128)S(1)} %bitcast.98), channel_id=1, source_target_pairs={{16,0},{32,16},{48,32},{64,48},{80,64},{96,80},{112,96},{128,112},... | collective-permute-start | bytes 503816 | tf_op jit(solution)/shard_map/ppermute | solution.py:15
  44.5 4.7 %copy-start.4 = (bf16[2,2,256,128]{3,2,1,0:T(8,128)(2,1)S(1)}, bf16[2,2,256,128]{3,2,1,0:T(8,128)(2,1)}, u32[]{:S(2)}) copy-start(bf16[2,2,256,128]{3,2,1,0:T(8,128)(2,1)} %param.17) | copy-start | bytes 786436
  54.1 2.7 %copy-start.2 = (bf16[2,80,1024]{2,1,0:T(8,128)(2,1)S(1)}, bf16[2,80,1024]{2,1,0:T(8,128)(2,1)}, u32[]{:S(2)}) copy-start(bf16[2,80,1024]{2,1,0:T(8,128)(2,1)} %param.10) | copy-start | bytes 983044
  56.9 1.7 copy-start.1
  56.9 1.7 copy-start.3
  59.3 2.3 %copy-start.8 = (f32[2,1024]{1,0:T(2,128)S(1)}, f32[2,1024]{1,0:T(2,128)}, u32[]{:S(2)}) copy-start(f32[2,1024]{1,0:T(2,128)} %param.9) | copy-start | bytes 24580
  61.6 3.9 %copy-start.6 = (f32[8,512,1]{0,2,1:T(1,128)S(1)}, f32[8,512,1]{0,2,1:T(1,128)}, u32[]{:S(2)}) copy-start(f32[8,512,1]{0,2,1:T(1,128)} %copy.72) | copy-start | bytes 49156
  65.5 63.0 %copy-start.7 = (bf16[2,80,32]{1,2,0:T(8,128)(2,1)S(1)}, bf16[2,80,32]{1,2,0:T(8,128)(2,1)}, u32[]{:S(2)}) copy-start(bf16[2,80,32]{1,2,0:T(8,128)(2,1)} %param.11) | copy-start | bytes 30724
  65.5 64.0 %copy-start.9 = (bf16[2,32]{1,0:T(2,128)(2,1)S(1)}, bf16[2,32]{1,0:T(2,128)(2,1)}, u32[]{:S(2)}) copy-start(bf16[2,32]{1,0:T(2,128)(2,1)} %param.13) | copy-start | bytes 388
  65.5 64.0 %copy-start.10 = (bf16[2,32]{1,0:T(2,128)(2,1)S(1)}, bf16[2,32]{1,0:T(2,128)(2,1)}, u32[]{:S(2)}) copy-start(bf16[2,32]{1,0:T(2,128)(2,1)} %param.12) | copy-start | bytes 388
  146.9 8.9 %collective-permute-start.2 = (f32[1,82,512]{1,2,0:T(8,128)S(1)}, f32[1,82,512]{1,2,0:T(8,128)S(1)}, u32[]{:S(2)}, u32[]{:S(2)}) collective-permute-start(f32[1,82,512]{1,2,0:T(8,128)S(1)} %bitcast.100), channel_id=1, source_target_pairs={{0,16},{16,32},{32,48},{48,64},{64,80},{80,96},{96,112},{112,128},... | collective-permute-start | bytes 503816 | tf_op jit(solution)/shard_map/ppermute | solution.py:12
  150.3 9.3 %collective-permute-start.3 = (f32[1,82,512]{1,2,0:T(8,128)S(1)}, f32[1,82,512]{1,2,0:T(8,128)S(1)}, u32[]{:S(2)}, u32[]{:S(2)}) collective-permute-start(f32[1,82,512]{1,2,0:T(8,128)S(1)} %bitcast.101), channel_id=1, source_target_pairs={{16,0},{32,16},{48,32},{64,48},{80,64},{96,80},{112,96},{128,112},... | collective-permute-start | bytes 503816 | tf_op jit(solution)/shard_map/ppermute | solution.py:15
  159.7 4.1 %copy-start.5 = (bf16[2,2,256,128]{3,2,1,0:T(8,128)(2,1)S(1)}, bf16[2,2,256,128]{3,2,1,0:T(8,128)(2,1)}, u32[]{:S(2)}) copy-start(bf16[2,2,256,128]{3,2,1,0:T(8,128)(2,1)} %param.17) | copy-start | bytes 786436
  171.4 1.6 copy-start
Sparse Core Ops, SparseCore 0:
  70.3 58.1 reduce-scatter.1
where the time goes:
time: 183 us; the launch traced here: 182 us
  waiting for transfers between devices  67.7 us (37%)
  blocking collectives  38.6 us (21%)
  local copies, waits for them, and re-layouts  37.8 us (21%)
  between operations  14.4 us (8%)
  starting transfers between devices  8.27 us (5%)
  other arithmetic  7.66 us (4%)
  matrix products  7.15 us (4%)
    reduce_scatter x1, waiting for transfers between devices, local(): lax.psum_scatter(increment_term, 'obs', scatter_dimension=1, tiled=True)  58.3 us
    all_gather x2, blocking collectives, local(): gathered = lax.all_gather(package[None], 'obs', axis=2, tiled=True)  38.6 us
    mul x6, local copies, waits for them, and re-layouts, update_block(): taper_levels * anom_coef * proj_levels  8.41 us
    gather x2, local copies, waits for them, and re-layouts, local(): picked = beside_all[region_off, :, region_slot]  7.32 us
    mul x6, local copies, waits for them, and re-layouts, update_block(): taper_levels * mean_coef * proj_levels  6.43 us
    ppermute x2, starting transfers between devices, extended(): lax.ppermute(lax.slice_in_dim(block, block.shape[dim] - width, None, axis...  5.46 us
    ppermute x2, waiting for transfers between devices, extended(): lax.ppermute(lax.slice_in_dim(block, 0, width, axis=dim), axis, backward)  5.36 us
    unnamed x29, local copies, waits for them, and re-layouts  4.72 us
  transfers between devices with their start and end apart: 5, of which 4 were waited for; matrix products, arithmetic and copies ran while one was open for 4% of the time, Pallas kernels for 0%

commit v1 on v0

v1 whole, which is shorter than its diff:
```python
import functools

import jax
import jax.numpy as jnp
from jax import lax
from jax.experimental import pallas as pl
from jax.experimental.pallas import tpu as pltpu
from jax.sharding import Mesh
from jax.sharding import PartitionSpec as P

F32 = jnp.float32
BF16 = jnp.bfloat16
LANES = 128
VMEM = pl.BlockSpec(memory_space=pltpu.VMEM)
SMEM = pl.BlockSpec(memory_space=pltpu.SMEM)
PARAMS = pltpu.CompilerParams(vmem_limit_bytes=24 * 1024 * 1024)


def dot(a, b, contract=((1,), (0,))):
    return lax.dot_general(a, b, (contract, ((), ())), preferred_element_type=F32)


def iota(shape, dim):
    return lax.broadcasted_iota(jnp.int32, shape, dim)


def one_hot(mask):
    return jnp.where(mask, 1.0, 0.0).astype(BF16)


def identity(size):
    return one_hot(iota((size, size), 0) == iota((size, size), 1))


def pack_kernel(prior_ref, value_ref, var_ref, first_ref, second_ref):
    _, members, width = prior_ref.shape
    row = iota((16, width), 0)
    value = value_ref[...].astype(F32)
    var = var_ref[...].astype(F32)
    tail = jnp.where(row == 0, value[0:1], 0.0)
    tail = jnp.where(row == 1, var[0:1], tail)
    tail = jnp.where(row == 2, value[1:2], tail)
    tail = jnp.where(row == 3, var[1:2], tail).astype(BF16)
    rest = jnp.zeros((LANES - members - 16, width), BF16)
    blank = jnp.zeros((16, width), BF16)
    turn = identity(width)
    first = jnp.concatenate([prior_ref[0], tail, rest], axis=0)
    second = jnp.concatenate([prior_ref[1], blank, rest], axis=0)
    first_ref[...] = dot(turn, first, ((1,), (1,))).astype(BF16)
    second_ref[...] = dot(turn, second, ((1,), (1,))).astype(BF16)


def pick(fields, ids):
    slots = fields.shape[1]
    step = 512
    total = None
    for start in range(0, slots, step):
        chosen = one_hot(iota((step, ids.shape[1]), 0) + start == ids)
        part = dot(fields[:, start : start + step], chosen)
        total = part if total is None else total + part
    return total


def package(ensemble, value, var):
    members = ensemble.shape[0]
    centre = jnp.sum(ensemble, axis=0, keepdims=True) / members
    anomaly = ensemble - centre
    spread = jnp.sum(anomaly * anomaly, axis=0, keepdims=True) / (members - 1)
    gain = 1.0 / (spread + var)
    factor = 1.0 / (1.0 + jnp.sqrt(var * gain))
    coef_anom = factor * gain / (members - 1)
    coef_mean = gain * (value - centre) / (members - 1)
    return anomaly, coef_anom, coef_mean


def update_tile(picked, members, value_row, mean_ref, anom_ref, taper_ref, colour, tile, new_mean_ref, new_anom_ref, change_ref):
    value = picked[value_row : value_row + 1]
    var = picked[value_row + 1 : value_row + 2]
    anomaly, coef_anom, coef_mean = package(picked[:members], value, var)
    basis = anomaly.astype(BF16)
    listed = basis.shape[1]
    coefs = jnp.concatenate([coef_anom, coef_mean, jnp.zeros((6, listed), F32)], axis=0).T
    taper = taper_ref[colour, tile].astype(F32)
    taper_anom = taper * coefs[:, 0:1]
    taper_mean = taper * coefs[:, 1:2]
    width = taper.shape[1]
    step = 2 * width
    for start in range(0, anom_ref.shape[2], step):
        cells = slice(start, start + step)
        anom = anom_ref[tile, :, cells]
        projection = dot(basis, anom, ((0,), (0,)))
        low, high = projection[:, :width], projection[:, width:]
        scaled = jnp.concatenate([(taper_anom * low).astype(BF16), (taper_anom * high).astype(BF16)], axis=1)
        shift_mean = jnp.concatenate(
            [jnp.sum(taper_mean * low, axis=0, keepdims=True), jnp.sum(taper_mean * high, axis=0, keepdims=True)], axis=1
        )
        mean = mean_ref[tile : tile + 1, cells]
        new_mean = mean + shift_mean
        new_mean_ref[tile : tile + 1, cells] = new_mean
        old = anom.astype(F32)
        new_anom = (old - dot(basis, scaled)).astype(BF16)
        new_anom_ref[tile, :, cells] = new_anom
        if change_ref is not None:
            change = (new_anom.astype(F32) - old + (new_mean - mean)).astype(BF16)
            for part in range(2):
                change_ref[start // width + part, :, tile * width : (tile + 1) * width] = change[
                    :, part * width : (part + 1) * width
                ]


def first_kernel(
    place_ref, records_ref, lists_ref, home_ref, weight_ref, mean_ref, anom_ref, taper_ref,
    new_mean_ref, new_anom_ref, prior_ref, errors_ref, rows_ref, change_ref,
):
    tiles, members, _ = anom_ref.shape
    chips = records_ref.shape[1]
    width = records_ref.shape[2] // 4
    region = 2 * chips * width
    for chip in range(chips):
        at = chip * 2 * width
        rows_ref[at : at + 2 * width] = records_ref[0, chip, : 2 * width]
        rows_ref[2 * region + at : 2 * region + at + 2 * width] = records_ref[1, chip, : 2 * width]
        for core in range(2):
            here = at + core * width
            rows_ref[region + here : region + here + width] = records_ref[core, chip, 2 * width : 3 * width]
            rows_ref[3 * region + here : 3 * region + here + width] = records_ref[core, chip, 3 * width :]
    turn = identity(LANES)
    fields = dot(turn, rows_ref[...], ((1,), (1,)))
    listed = fields[: members + 16, : 3 * region].astype(BF16)
    errors_ref[...] = listed[members:]
    base = place_ref[0] * region
    for tile in range(tiles):
        picked = pick(listed, lists_ref[0, tile : tile + 1] - base)
        update_tile(
            picked, members, members, mean_ref, anom_ref, taper_ref, 0, tile, new_mean_ref, new_anom_ref, change_ref
        )
    home = home_ref[...] - place_ref[1]
    columns = change_ref.shape[2]
    at_home = one_hot(iota((columns, region), 0) == home)
    prior = fields[:members, 3 * region :]
    increment = None
    for level in range(change_ref.shape[0]):
        part = dot(change_ref[level], at_home) * weight_ref[level : level + 1]
        increment = part if increment is None else increment + part
    inside = (home >= 0) & (home < columns)
    updated = jnp.where(inside, prior + increment, 0.0).astype(BF16)
    half = region // 2
    prior_ref[0] = updated[:, :half]
    prior_ref[1] = updated[:, half:]


def second_kernel(
    place_ref, own_ref, beside_ref, errors_ref, lists_ref, mean_ref, anom_ref, taper_ref, new_mean_ref, new_anom_ref
):
    tiles, members, _ = anom_ref.shape
    ensemble = jnp.concatenate(
        [beside_ref[0, 0], beside_ref[0, 1], own_ref[0], own_ref[1], beside_ref[1, 0], beside_ref[1, 1]], axis=1
    )
    listed = jnp.concatenate([ensemble, errors_ref[...]], axis=0)
    region = own_ref.shape[0] * own_ref.shape[2]
    base = place_ref[0] * region
    for tile in range(tiles):
        picked = pick(listed, lists_ref[1, tile : tile + 1] - base)
        update_tile(
            picked, members, members + 2, mean_ref, anom_ref, taper_ref, 1, tile, new_mean_ref, new_anom_ref, None
        )


def beside(rows, chips, states):
    pairs = []
    for state in range(states):
        for chip in range(chips):
            if state + 1 < states:
                pairs.append(((state * chips + chip) * 2, ((state + 1) * chips + chip) * 2))
            if state > 0:
                pairs.append(((state * chips + chip) * 2 + 1, ((state - 1) * chips + chip) * 2 + 1))
    return lax.ppermute(rows, ("state", "chip", "core"), pairs)


def local(state_mean, state_anom, obs_prior, obs_value, obs_var, obs_weight, obs_home, tile_obs, taper):
    tiles, members, cells = state_anom.shape
    tile_width = taper.shape[3]
    chips, states = lax.axis_size("chip"), lax.axis_size("state")
    width = obs_prior.shape[2]
    region = 2 * chips * width
    state, chip, core = lax.axis_index("state"), lax.axis_index("chip"), lax.axis_index("core")
    first_column = ((state * chips + chip) * 2 + core) * tiles * tile_width
    place = jnp.stack([state - 1, first_column]).astype(jnp.int32)

    block = jax.ShapeDtypeStruct((width, LANES), BF16)
    first, second = pl.pallas_call(
        pack_kernel, out_shape=(block, block), in_specs=[VMEM] * 3, out_specs=(VMEM, VMEM), name="pack"
    )(obs_prior, obs_value, obs_var)
    pair = lax.all_gather(first, "core", axis=0, tiled=True)
    near = beside(pair, chips, states)
    sent = jnp.concatenate([near, first, second], axis=0)
    sent = jnp.broadcast_to(sent[None], (chips, 4 * width, LANES))
    got = lax.all_to_all(sent, "chip", 0, 0)
    records = lax.all_gather(got, "core", axis=0)

    state_shapes = (
        jax.ShapeDtypeStruct(state_mean.shape, state_mean.dtype),
        jax.ShapeDtypeStruct(state_anom.shape, state_anom.dtype),
    )
    new_mean, new_anom, priors, errors = pl.pallas_call(
        first_kernel,
        out_shape=state_shapes
        + (
            jax.ShapeDtypeStruct((2, members, region // 2), BF16),
            jax.ShapeDtypeStruct((16, 3 * region), BF16),
        ),
        in_specs=[SMEM] + [VMEM] * 7,
        out_specs=(VMEM,) * 4,
        scratch_shapes=[
            pltpu.VMEM((4 * region, LANES), BF16),
            pltpu.VMEM((cells // tile_width, members, tiles * tile_width), BF16),
        ],
        compiler_params=PARAMS,
        name="first",
    )(place, records, tile_obs, obs_home[None], obs_weight, state_mean, state_anom, taper)

    shared = lax.all_gather(priors, "core", axis=0)
    half = lax.dynamic_index_in_dim(shared, core, axis=1, keepdims=False)
    half = half[0] + half[1]
    halves = lax.all_to_all(jnp.broadcast_to(half[None], (chips,) + half.shape), "chip", 0, 0)
    total = jnp.sum(halves, axis=0, dtype=BF16)
    own = lax.all_gather(total, "core", axis=0)
    sides = lax.all_gather(beside(own, chips, states), "core", axis=0)

    return pl.pallas_call(
        second_kernel,
        out_shape=state_shapes,
        in_specs=[SMEM] + [VMEM] * 7,
        out_specs=(VMEM,) * 2,
        compiler_params=PARAMS,
        name="second",
    )(place, own, sides, errors, tile_obs, new_mean, new_anom, taper)


def solution(mesh):
    states, columns = mesh.shape["state"], mesh.shape["obs"]
    fine = Mesh(mesh.devices.reshape(states, columns // 2, 2), ("state", "chip", "core"))
    every = ("state", "chip", "core")
    in_specs = (
        P(every, None),
        P(every, None, None),
        P(None, None, every),
        P(None, every),
        P(None, every),
        P(None, "state"),
        P("state"),
        P(None, every, None),
        P(None, every, None, None),
    )
    out_specs = (P(every, None), P(every, None, None))
    return jax.shard_map(local, mesh=fine, in_specs=in_specs, out_specs=out_specs, check_vma=False)
```

time: 183 us -> 79.2 us (0.43)
  the two profiles are of different devices: /device:TPU:1 before, /device:TPU:7 now
where the time goes in v1:
time: 79.2 us; the launch traced here: 78.6 us
  blocking collectives  30.8 us (39%)
  starting transfers between devices  23.5 us (30%)
  waiting for transfers between devices  11.9 us (15%)
  Pallas kernels  8.76 us (11%)
  local copies, waits for them, and re-layouts  2.86 us (4%)
    ppermute x2, starting transfers between devices, beside(): return lax.ppermute(rows, ('state', 'chip', 'core'), pairs)  16.6 us
    all_to_all x1, blocking collectives, local(): lax.all_to_all(jnp.broadcast_to(half[None], (chips,) + half.shape), 'chip...  16.1 us
    all_to_all x1, waiting for transfers between devices, local(): got = lax.all_to_all(sent, 'chip', 0, 0)  9.57 us
    all_to_all x1, starting transfers between devices, local(): got = lax.all_to_all(sent, 'chip', 0, 0)  6.82 us
    all_gather x1, blocking collectives, local(): records = lax.all_gather(got, 'core', axis=0)  5.11 us
    pallas_call x1, Pallas kernels, local(): pl.pallas_call(first_kernel, out_shape=state_shapes + (jax.ShapeDtypeStru...  3.64 us
    pallas_call x1, Pallas kernels, local(): pl.pallas_call(second_kernel, out_shape=state_shapes, in_specs=[SMEM] + [...  3.58 us
    all_gather x1, blocking collectives, local(): sides = lax.all_gather(beside(own, chips, states), 'core', axis=0)  3.14 us
  transfers between devices with their start and end apart: 3, of which 3 were waited for; matrix products, arithmetic and copies ran while one was open for 0% of the time, Pallas kernels for 0%

profile of v1, /device:TPU:7, one launch (start us, length us, event | category | flops | bytes accessed | tf_op | source)
XLA Modules:
  0.0 78.6 jit_solution(6015222204301729921)
XLA Ops:
  0.6 1.4 %copy.13.prior_ref = bf16[2,80,32]{2,1,0:T(8,128)(2,1)} copy(bf16[2,80,32]{1,2,0:T(8,128)(2,1)} %param.11) | data formatting | bytes 20480 | tf_op args[2]
  2.1 1.5 %pack.1 = (bf16[32,128]{1,0:T(8,128)(2,1)}, bf16[32,128]{1,0:T(8,128)(2,1)}) custom-call(bf16[2,80,32]{2,1,0:T(8,128)(2,1)} %copy.13.prior_ref, bf16[2,32]{1,0:T(2,128)(2,1)} %value_ref.1, bf16[2,32]{1,0:T(2,128)(2,1)} %var_ref.1), custom_call_target="tpu_custom_call" | custom-call | tf_op jit(solution)/shard_map/pack/pallas_call | solution.py:191
  3.6 2.5 %all_gather.27 = bf16[64,128]{1,0:T(8,128)(2,1)S(1)} all-gather(bf16[32,128]{1,0:T(8,128)(2,1)} %get-tuple-element.8), channel_id=1, replica_groups=mesh['state'=32,'chip'=8,'core'=2] {'core'}, dimensions={0}, use_global_device_ids=true | all-gather | bytes 24576 | tf_op jit(solution)/shard_map/all_gather | solution.py:194
  6.1 10.9 %collective-permute-start = (bf16[64,128]{1,0:T(8,128)(2,1)S(1)}, bf16[64,128]{1,0:T(8,128)(2,1)S(1)}, u32[]{:S(2)}, u32[]{:S(2)}) collective-permute-start(bf16[64,128]{1,0:T(8,128)(2,1)S(1)} %all_gather.27), channel_id=1, source_target_pairs={{0,16},{2,18},{4,20},{6,22},{8,24},{10,26},{12,28},{14,30},{16,32}... | collective-permute-start | bytes 49160 | tf_op jit(solution)/shard_map/ppermute | solution.py:177
  17.0 0.8 %collective-permute-done = bf16[64,128]{1,0:T(8,128)(2,1)S(1)} collective-permute-done((bf16[64,128]{1,0:T(8,128)(2,1)S(1)}, bf16[64,128]{1,0:T(8,128)(2,1)S(1)}, u32[]{:S(2)}, u32[]{:S(2)}) %collective-permute-start) | collective-permute-done | bytes 16416 | tf_op jit(solution)/shard_map/ppermute | solution.py:177
  17.9 0.0 copy-done.6
  17.9 0.0 copy-done.7
  17.9 0.7 broadcast_in_dim.6
  18.6 6.8 %all-to-all-start = ((bf16[8,128,128]{2,1,0:T(8,128)(2,1)}), bf16[8,128,128]{2,1,0:T(8,128)(2,1)S(1)}, u32[]{:S(2)}, u32[]{:S(2)}) async-start(bf16[8,128,128]{2,1,0:T(8,128)(2,1)} %broadcast_in_dim.6), calls=%async_computation | async-start | bytes 524288 | tf_op jit(solution)/shard_map/all_to_all | solution.py:198
  25.4 0.1 pad_add_fusion.place_ref
  25.5 9.6 %all-to-all-done = bf16[8,128,128]{2,1,0:T(8,128)(2,1)S(1)} async-done(((bf16[8,128,128]{2,1,0:T(8,128)(2,1)}), bf16[8,128,128]{2,1,0:T(8,128)(2,1)S(1)}, u32[]{:S(2)}, u32[]{:S(2)}) %all-to-all-start) | async-done | bytes 262176 | tf_op jit(solution)/shard_map/all_to_all | solution.py:198
  35.1 5.1 %all-gather = bf16[16,128,128]{2,1,0:T(8,128)(2,1)S(1)} all-gather(bf16[8,128,128]{2,1,0:T(8,128)(2,1)S(1)} %all-to-all-done), channel_id=2, replica_groups=mesh['state'=32,'chip'=8,'core'=2] {'core'}, dimensions={0}, use_global_device_ids=true | all-gather | bytes 786432 | tf_op jit(solution)/shard_map/all_gather | solution.py:199
  40.2 0.0 copy-done
  40.2 0.0 copy-done.1
  40.2 0.0 copy-done.2
  40.2 0.6 copy-done.5
  40.9 3.6 %first.1 = (f32[2,1024]{1,0:T(2,128)S(1)}, bf16[2,80,1024]{2,1,0:T(8,128)(2,1)S(1)}, bf16[2,80,256]{2,1,0:T(8,128)(2,1)S(1)}, bf16[16,1536]{1,0:T(8,128)(2,1)S(1)}) custom-call(s32[2]{0:T(128)S(1)} %pad_add_fusion.place_ref, bf16[2,8,128,128]{3,2,1,0:T(8,128)(2,1)S(1)} %bitcast.9, s32[2,2,256]{2,1,0:T(2,128)S(1)} %copy-done.3, s32[1,512]{1,0:T(1,128)S(1)} %bitcast.13, ...), custom_call_target="tpu_custom_call" | custom-call | tf_op jit(solution)/shard_map/first/pallas_call | solution.py:205
  44.5 1.9 %all-gather.1 = bf16[4,80,256]{2,1,0:T(8,128)(2,1)S(1)} all-gather(bf16[2,80,256]{2,1,0:T(8,128)(2,1)S(1)} %get-tuple-element.10), channel_id=3, replica_groups=mesh['state'=32,'chip'=8,'core'=2] {'core'}, dimensions={0}, use_global_device_ids=true | all-gather | bytes 245760 | tf_op jit(solution)/shard_map/all_gather | solution.py:222
  46.5 16.1 %all_to_all.10 = bf16[8,80,256]{2,1,0:T(8,128)(2,1)S(1)} all-to-all(bf16[8,80,256]{2,1,0:T(8,128)(2,1)S(1)} %broadcast_in_dim.8), channel_id=1, replica_groups=mesh['state'=32,'chip'=8,'core'=2] {'chip'}, dimensions={0} | all-to-all | bytes 655360 | tf_op jit(solution)/shard_map/all_to_all | solution.py:225
  62.7 2.0 %all-gather.2 = bf16[160,256]{1,0:T(8,128)(2,1)S(1)} all-gather(bf16[80,256]{1,0:T(8,128)(2,1)S(1)} %reduce_sum.9), channel_id=4, replica_groups=mesh['state'=32,'chip'=8,'core'=2] {'core'}, dimensions={0}, use_global_device_ids=true | all-gather | bytes 122880 | tf_op jit(solution)/shard_map/all_gather | solution.py:227
  64.7 5.7 %collective-permute-start.1 = (bf16[2,80,256]{2,1,0:T(8,128)(2,1)S(1)}, bf16[2,80,256]{2,1,0:T(8,128)(2,1)S(1)}, u32[]{:S(2)}, u32[]{:S(2)}) collective-permute-start(bf16[2,80,256]{2,1,0:T(8,128)(2,1)S(1)} %bitcast.11), channel_id=1, source_target_pairs={{0,16},{2,18},{4,20},{6,22},{8,24},{10,26},{12,28},{14,30},{16,32}... | collective-permute-start | bytes 245768 | tf_op jit(solution)/shard_map/ppermute | solution.py:177
  70.4 1.5 %collective-permute-done.1 = bf16[2,80,256]{2,1,0:T(8,128)(2,1)S(1)} collective-permute-done((bf16[2,80,256]{2,1,0:T(8,128)(2,1)S(1)}, bf16[2,80,256]{2,1,0:T(8,128)(2,1)S(1)}, u32[]{:S(2)}, u32[]{:S(2)}) %collective-permute-start.1) | collective-permute-done | bytes 81952 | tf_op jit(solution)/shard_map/ppermute | solution.py:177
  71.9 3.1 %all-gather.3 = bf16[4,80,256]{2,1,0:T(8,128)(2,1)S(1)} all-gather(bf16[2,80,256]{2,1,0:T(8,128)(2,1)S(1)} %collective-permute-done.1), channel_id=5, replica_groups=mesh['state'=32,'chip'=8,'core'=2] {'core'}, dimensions={0}, use_global_device_ids=true | all-gather | bytes 245760 | tf_op jit(solution)/shard_map/all_gather | solution.py:228
  75.0 3.6 %second.1 = (f32[2,1024]{1,0:T(2,128)}, bf16[2,80,1024]{2,1,0:T(8,128)(2,1)}) custom-call(s32[2]{0:T(128)S(1)} %pad_add_fusion.place_ref, bf16[2,80,256]{2,1,0:T(8,128)(2,1)S(1)} %bitcast.12, bf16[2,2,80,256]{3,2,1,0:T(8,128)(2,1)S(1)} %bitcast.10, bf16[16,1536]{1,0:T(8,128)(2,1)S(1)} %get-tuple-element.11.errors_ref, s32[2,2,256]{2,1,0:T(2,128)S(1)} %copy-done.3, ...), custom_call_target="tpu_custom_call" | custom-call | tf_op jit(solution)/shard_map/second/pallas_call | solution.py:230
  (14 shorter events, 0.1 us)
Async XLA Ops:
  3.6 14.3 %copy-start.6 = (bf16[32,128]{1,0:T(8,128)(2,1)S(1)}, bf16[32,128]{1,0:T(8,128)(2,1)}, u32[]{:S(2)}) copy-start(bf16[32,128]{1,0:T(8,128)(2,1)} %get-tuple-element.8) | copy-start | bytes 24580
  3.6 14.3 %copy-start.7 = (bf16[32,128]{1,0:T(8,128)(2,1)S(1)}, bf16[32,128]{1,0:T(8,128)(2,1)}, u32[]{:S(2)}) copy-start(bf16[32,128]{1,0:T(8,128)(2,1)} %get-tuple-element.9) | copy-start | bytes 24580
  6.1 11.8 %collective-permute-start = (bf16[64,128]{1,0:T(8,128)(2,1)S(1)}, bf16[64,128]{1,0:T(8,128)(2,1)S(1)}, u32[]{:S(2)}, u32[]{:S(2)}) collective-permute-start(bf16[64,128]{1,0:T(8,128)(2,1)S(1)} %all_gather.27), channel_id=1, source_target_pairs={{0,16},{2,18},{4,20},{6,22},{8,24},{10,26},{12,28},{14,30},{16,32}... | collective-permute-start | bytes 49160 | tf_op jit(solution)/shard_map/ppermute | solution.py:177
  18.6 16.5 %all-to-all-start = ((bf16[8,128,128]{2,1,0:T(8,128)(2,1)}), bf16[8,128,128]{2,1,0:T(8,128)(2,1)S(1)}, u32[]{:S(2)}, u32[]{:S(2)}) async-start(bf16[8,128,128]{2,1,0:T(8,128)(2,1)} %broadcast_in_dim.6), calls=%async_computation | async-start | bytes 524288 | tf_op jit(solution)/shard_map/all_to_all | solution.py:198
  25.5 14.7 %copy-start = (bf16[2,2,256,128]{3,2,1,0:T(8,128)(2,1)S(1)}, bf16[2,2,256,128]{3,2,1,0:T(8,128)(2,1)}, u32[]{:S(2)}) copy-start(bf16[2,2,256,128]{3,2,1,0:T(8,128)(2,1)} %taper_ref.3) | copy-start | bytes 786436
  25.5 14.7 %copy-start.1 = (bf16[2,80,1024]{2,1,0:T(8,128)(2,1)S(1)}, bf16[2,80,1024]{2,1,0:T(8,128)(2,1)}, u32[]{:S(2)}) copy-start(bf16[2,80,1024]{2,1,0:T(8,128)(2,1)} %anom_ref.1) | copy-start | bytes 983044
  25.5 14.7 %copy-start.2 = (f32[8,512]{1,0:T(8,128)S(1)}, f32[8,512]{1,0:T(8,128)}, u32[]{:S(2)}) copy-start(f32[8,512]{1,0:T(8,128)} %weight_ref.1) | copy-start | bytes 49156
  35.1 5.1 %copy-start.3 = (s32[2,2,256]{2,1,0:T(2,128)S(1)}, s32[2,2,256]{2,1,0:T(2,128)}, u32[]{:S(2)}) copy-start(s32[2,2,256]{2,1,0:T(2,128)} %lists_ref.3) | copy-start | bytes 12292
  35.1 5.1 %copy-start.4 = (f32[2,1024]{1,0:T(2,128)S(1)}, f32[2,1024]{1,0:T(2,128)}, u32[]{:S(2)}) copy-start(f32[2,1024]{1,0:T(2,128)} %mean_ref.1) | copy-start | bytes 24580
  40.2 0.7 copy-start.5
  64.7 7.2 %collective-permute-start.1 = (bf16[2,80,256]{2,1,0:T(8,128)(2,1)S(1)}, bf16[2,80,256]{2,1,0:T(8,128)(2,1)S(1)}, u32[]{:S(2)}, u32[]{:S(2)}) collective-permute-start(bf16[2,80,256]{2,1,0:T(8,128)(2,1)S(1)} %bitcast.11), channel_id=1, source_target_pairs={{0,16},{2,18},{4,20},{6,22},{8,24},{10,26},{12,28},{14,30},{16,32}... | collective-permute-start | bytes 245768 | tf_op jit(solution)/shard_map/ppermute | solution.py:177

commit v2 on v1

v2 whole, which is shorter than its diff:
```python
import functools

import jax
import jax.numpy as jnp
from jax import lax
from jax.experimental import pallas as pl
from jax.experimental.pallas import tpu as pltpu
from jax.sharding import Mesh
from jax.sharding import PartitionSpec as P

F32 = jnp.float32
BF16 = jnp.bfloat16
LANES = 128
SLOTS = 128
VMEM = pl.BlockSpec(memory_space=pltpu.VMEM)
SMEM = pl.BlockSpec(memory_space=pltpu.SMEM)
PARAMS = pltpu.CompilerParams(vmem_limit_bytes=24 * 1024 * 1024)


def dot(a, b, contract=((1,), (0,))):
    return lax.dot_general(a, b, (contract, ((), ())), preferred_element_type=F32)


def iota(shape, dim):
    return lax.broadcasted_iota(jnp.int32, shape, dim)


def one_hot(mask):
    return jnp.where(mask, 1.0, 0.0).astype(BF16)


def identity(size):
    return one_hot(iota((size, size), 0) == iota((size, size), 1))


def pack_kernel(prior_ref, value_ref, var_ref, rows_ref):
    _, width, members = prior_ref.shape
    row = iota((LANES, width), 0) - members
    value = value_ref[...].astype(F32)
    var = var_ref[...].astype(F32)
    tail = jnp.where(row == 0, value[0:1], 0.0)
    tail = jnp.where(row == 1, var[0:1], tail)
    tail = jnp.where(row == 2, value[1:2], tail)
    tail = jnp.where(row == 3, var[1:2], tail).astype(BF16)
    spread = one_hot(iota((members, LANES), 0) == iota((members, LANES), 1))
    first = dot(prior_ref[0], spread) + dot(identity(width), tail, ((1,), (1,)))
    second = dot(prior_ref[1], spread)
    for copy in range(rows_ref.shape[0]):
        rows_ref[copy, 0] = first.astype(BF16)
        rows_ref[copy, 1] = second.astype(BF16)


def pick(fields, ids):
    slots = fields.shape[1]
    step = 512
    total = None
    for start in range(0, slots, step):
        chosen = one_hot(iota((step, ids.shape[1]), 0) + start == ids)
        part = dot(fields[:, start : start + step], chosen)
        total = part if total is None else total + part
    return total


def package(ensemble, value, var):
    members = ensemble.shape[0]
    centre = jnp.sum(ensemble, axis=0, keepdims=True) / members
    anomaly = ensemble - centre
    spread = jnp.sum(anomaly * anomaly, axis=0, keepdims=True) / (members - 1)
    gain = 1.0 / (spread + var)
    factor = 1.0 / (1.0 + jnp.sqrt(var * gain))
    coef_anom = factor * gain / (members - 1)
    coef_mean = gain * (value - centre) / (members - 1)
    return anomaly, coef_anom, coef_mean


def scale_tile(picked, members, value_row, mean_ref, anom_ref, taper_ref, colour, tile, new_mean_ref, scaled_ref):
    value = picked[value_row : value_row + 1]
    var = picked[value_row + 1 : value_row + 2]
    anomaly, coef_anom, coef_mean = package(picked[:members], value, var)
    basis = anomaly.astype(BF16)
    listed = basis.shape[1]
    coefs = jnp.concatenate([coef_anom, coef_mean, jnp.zeros((6, listed), F32)], axis=0).T
    taper = taper_ref[colour, tile].astype(F32)
    taper_anom = taper * coefs[:, 0:1]
    taper_mean = taper * coefs[:, 1:2]
    width = taper.shape[1]
    step = 2 * width
    for start in range(0, anom_ref.shape[2], step):
        projection = dot(basis, anom_ref[tile, :, start : start + step], ((0,), (0,)))
        for part in range(0, step, width):
            cells = slice(start + part, start + part + width)
            level = projection[:, part : part + width]
            scaled_ref[tile, :, cells] = (taper_anom * level).astype(BF16)
            shift = jnp.sum(taper_mean * level, axis=0, keepdims=True)
            new_mean_ref[tile : tile + 1, cells] = mean_ref[tile : tile + 1, cells] + shift
    return basis


def shift_tile(basis, mean_ref, anom_ref, tile, new_mean_ref, new_anom_ref, scaled_ref, width, change_ref):
    step = 2 * width
    for start in range(0, anom_ref.shape[2], step):
        cells = slice(start, start + step)
        old = anom_ref[tile, :, cells].astype(F32)
        new_anom = (old - dot(basis, scaled_ref[tile, :, cells])).astype(BF16)
        new_anom_ref[tile, :, cells] = new_anom
        if change_ref is not None:
            rise = new_mean_ref[tile : tile + 1, cells] - mean_ref[tile : tile + 1, cells]
            change = (new_anom.astype(F32) - old + rise).astype(BF16)
            for part in range(2):
                change_ref[start // width + part, :, tile * width : (tile + 1) * width] = change[
                    :, part * width : (part + 1) * width
                ]


def update_tiles(
    listed, lists_ref, colour, base, members, value_row, mean_ref, anom_ref, taper_ref,
    new_mean_ref, new_anom_ref, scaled_ref, change_ref,
):
    bases = []
    for tile in range(anom_ref.shape[0]):
        picked = pick(listed, lists_ref[colour, tile : tile + 1] - base)
        bases.append(
            scale_tile(
                picked, members, value_row, mean_ref, anom_ref, taper_ref, colour, tile, new_mean_ref, scaled_ref
            )
        )
    for tile, basis in enumerate(bases):
        shift_tile(
            basis, mean_ref, anom_ref, tile, new_mean_ref, new_anom_ref, scaled_ref, taper_ref.shape[3], change_ref
        )


def plan_kernel(chips, chip_columns, place_ref, home_ref, slot_ref, near_ref, crowded_ref):
    region = home_ref.shape[1]
    column = home_ref[...] - place_ref[2]
    near_ref[...] = home_ref[...] - place_ref[1]
    chip = jnp.zeros_like(column)
    for edge in range(1, chips):
        chip = chip + jnp.where(column >= edge * chip_columns, 1, 0)
    chip = chip.astype(F32)
    across = jnp.broadcast_to(chip, (8, region)).T[:, 0:1]
    earlier = (across == chip) & (iota((region, region), 0) < iota((region, region), 1))
    rank = jnp.sum(jnp.where(earlier, 1.0, 0.0), axis=0, keepdims=True)
    slot_ref[...] = (chip * SLOTS + rank).astype(jnp.int32)
    crowded_ref[0] = (jnp.max(rank) >= SLOTS).astype(jnp.int32)


def first_kernel(
    place_ref, row_ref, beside_ref, lists_ref, home_ref, slot_ref, weight_ref, mean_ref, anom_ref, taper_ref,
    new_mean_ref, new_anom_ref, packed_ref, prior_ref, errors_ref, rows_ref, scaled_ref, change_ref,
):
    members = anom_ref.shape[1]
    _, chips, _, width, _ = row_ref.shape
    region = 2 * chips * width
    for chip in range(chips):
        for core in range(2):
            at = (chip * 2 + core) * width
            for part, block in enumerate(
                (beside_ref[0, 0, core, chip], row_ref[core, chip, 0], beside_ref[1, 1, core, chip], row_ref[core, chip, 1])
            ):
                rows_ref[part * region + at : part * region + at + width] = block
    turn = identity(LANES)
    fields = dot(turn, rows_ref[...], ((1,), (1,)))
    listed = fields[: members + 16, : 3 * region].astype(BF16)
    errors_ref[...] = listed[members:]
    base = place_ref[0] * region
    update_tiles(
        listed, lists_ref, 0, base, members, members, mean_ref, anom_ref, taper_ref,
        new_mean_ref, new_anom_ref, scaled_ref, change_ref,
    )
    home = home_ref[...]
    columns = change_ref.shape[2]
    at_home = one_hot(iota((columns, region), 0) == home)
    prior = fields[:members, 3 * region :]
    increment = None
    for level in range(change_ref.shape[0]):
        part = dot(change_ref[level], at_home) * weight_ref[level : level + 1]
        increment = part if increment is None else increment + part
    inside = (home >= 0) & (home < columns)
    updated = jnp.where(inside, prior + increment, 0.0).astype(BF16)
    prior_ref[...] = updated
    to_slot = one_hot(iota((SLOTS, region), 0) + place_ref[3] * SLOTS == slot_ref[...])
    packed_ref[...] = dot(updated, to_slot, ((1,), (1,))).astype(BF16)


def spread_kernel(packed_ref, slot_ref, prior_ref):
    region = slot_ref.shape[1]
    total = None
    for chip in range(packed_ref.shape[0]):
        from_slot = one_hot(iota((SLOTS, region), 0) + chip * SLOTS == slot_ref[...])
        part = dot(packed_ref[chip], from_slot)
        total = part if total is None else total + part
    prior_ref[...] = total.astype(BF16)


def second_kernel(
    place_ref, own_ref, beside_ref, errors_ref, lists_ref, mean_ref, anom_ref, taper_ref,
    new_mean_ref, new_anom_ref, scaled_ref,
):
    members = anom_ref.shape[1]
    ensemble = jnp.concatenate([beside_ref[0, 0], own_ref[...], beside_ref[1, 1]], axis=1)
    listed = jnp.concatenate([ensemble, errors_ref[...]], axis=0)
    base = place_ref[0] * own_ref.shape[1]
    update_tiles(
        listed, lists_ref, 1, base, members, members + 2, mean_ref, anom_ref, taper_ref,
        new_mean_ref, new_anom_ref, scaled_ref, None,
    )


def beside(rows, chips, states):
    at = lambda state, chip, core: (state * chips + chip) * 2 + core
    groups = [[at(s, c, 1), at(s + 1, c, 0)] for s in range(states - 1) for c in range(chips)]
    for state, core in ((0, 0), (states - 1, 1)):
        groups += [[at(state, c, core), at(state, c + 1, core)] for c in range(0, chips, 2)]
    swapped = lax.all_gather(rows, ("state", "chip", "core"), axis_index_groups=groups)
    return lax.all_gather(swapped, "core")


def local(state_mean, state_anom, obs_prior, obs_value, obs_var, obs_weight, obs_home, tile_obs, taper):
    tiles, members, cells = state_anom.shape
    tile_width = taper.shape[3]
    chips, states = lax.axis_size("chip"), lax.axis_size("state")
    width = obs_prior.shape[2]
    region = 2 * chips * width
    state, chip, core = lax.axis_index("state"), lax.axis_index("chip"), lax.axis_index("core")
    chip_columns = 2 * tiles * tile_width
    row_column = state * chips * chip_columns
    first_column = row_column + chip * chip_columns + core * tiles * tile_width
    place = jnp.stack([state - 1, first_column, row_column, chip]).astype(jnp.int32)

    sent = pl.pallas_call(
        pack_kernel,
        out_shape=jax.ShapeDtypeStruct((chips, 2, width, LANES), BF16),
        in_specs=[VMEM] * 3,
        out_specs=VMEM,
        name="pack",
    )(jnp.swapaxes(obs_prior, 1, 2), obs_value, obs_var)
    row = lax.all_gather(lax.all_to_all(sent, "chip", 0, 0), "core", axis=0)
    near = beside(row[:, :, 0], chips, states)

    slot, home, crowded = pl.pallas_call(
        functools.partial(plan_kernel, chips, chip_columns),
        out_shape=(jax.ShapeDtypeStruct((1, region), jnp.int32),) * 2 + (jax.ShapeDtypeStruct((1,), jnp.int32),),
        in_specs=[SMEM, VMEM],
        out_specs=(VMEM, VMEM, SMEM),
        name="plan",
    )(place, obs_home[None])

    state_shapes = (
        jax.ShapeDtypeStruct(state_mean.shape, state_mean.dtype),
        jax.ShapeDtypeStruct(state_anom.shape, state_anom.dtype),
    )
    scaled = pltpu.VMEM((tiles, tile_obs.shape[2], cells), BF16)
    prior_shape = jax.ShapeDtypeStruct((members, region), BF16)
    new_mean, new_anom, packed, prior, errors = pl.pallas_call(
        first_kernel,
        out_shape=state_shapes
        + (
            jax.ShapeDtypeStruct((members, SLOTS), BF16),
            prior_shape,
            jax.ShapeDtypeStruct((16, 3 * region), BF16),
        ),
        in_specs=[SMEM] + [VMEM] * 9,
        out_specs=(VMEM,) * 5,
        scratch_shapes=[
            pltpu.VMEM((4 * region, LANES), BF16),
            scaled,
            pltpu.VMEM((cells // tile_width, members, tiles * tile_width), BF16),
        ],
        compiler_params=PARAMS,
        name="first",
    )(place, row, near, tile_obs, home, slot, obs_weight, state_mean, state_anom, taper)

    def to_row(part):
        both = lax.all_gather(part, "core", axis=0)
        both = both[0] + both[1]
        return lax.all_to_all(jnp.broadcast_to(both[None], (chips,) + both.shape), "chip", 0, 0)

    def by_slot(packed, prior, slot):
        return pl.pallas_call(
            spread_kernel, out_shape=prior_shape, in_specs=[VMEM] * 2, out_specs=VMEM, name="spread"
        )(to_row(packed), slot)

    def whole(packed, prior, slot):
        return jnp.sum(to_row(prior), axis=0, dtype=BF16)

    own = lax.cond(crowded[0] == 0, by_slot, whole, packed, prior, slot)
    sides = beside(own, chips, states)

    return pl.pallas_call(
        second_kernel,
        out_shape=state_shapes,
        in_specs=[SMEM] + [VMEM] * 7,
        out_specs=(VMEM,) * 2,
        scratch_shapes=[scaled],
        compiler_params=PARAMS,
        name="second",
    )(place, own, sides, errors, tile_obs, new_mean, new_anom, taper)


def solution(mesh):
    states, columns = mesh.shape["state"], mesh.shape["obs"]
    fine = Mesh(mesh.devices.reshape(states, columns // 2, 2), ("state", "chip", "core"))
    every = ("state", "chip", "core")
    in_specs = (
        P(every, None),
        P(every, None, None),
        P(None, None, every),
        P(None, every),
        P(None, every),
        P(None, "state"),
        P("state"),
        P(None, every, None),
        P(None, every, None, None),
    )
    out_specs = (P(every, None), P(every, None, None))
    return jax.shard_map(local, mesh=fine, in_specs=in_specs, out_specs=out_specs, check_vma=False)
```

time: 79.2 us -> 67.9 us (0.86)
  starting transfers between devices: 23.5 us -> 6.82 us
  blocking collectives: 30.8 us -> 42.5 us
  waiting for transfers between devices: 11.9 us -> 4.93 us
  local copies, waits for them, and re-layouts: 2.86 us -> 0.71 us
  Pallas kernels: 8.76 us -> 10.5 us
    ppermute x2 -> x0, starting transfers between devices: 16.6 us -> none  [beside(): return lax.ppermute(rows, ('state', 'chip', 'core'), pairs)]
    all_gather x5 -> x6, blocking collectives: 14.7 us -> 30.3 us  [the longest x2 14.3 us: beside(): return lax.all_gather(swapped, 'core')]
    all_to_all x1, waiting for transfers between devices: 9.57 us -> 4.93 us  [local(): row = lax.all_gather(lax.all_to_all(sent, 'chip', 0, 0), 'core', axis=0)]
    all_to_all x1, blocking collectives: 16.1 us -> 12.3 us  [to_row(): lax.all_to_all(jnp.broadcast_to(both[None], (chips,) + both.shape), 'chip...]
    pallas_call x1 -> x3, Pallas kernels: 1.54 us -> 4.38 us  [the longest x1 1.6 us: local(): pl.pallas_call(functools.partial(plan_kernel, chips, chip_columns), out_s...]
    ppermute x2 -> x0, waiting for transfers between devices: 2.31 us -> none  [beside(): return lax.ppermute(rows, ('state', 'chip', 'core'), pairs)]
    unnamed x17 -> x14, local copies, waits for them, and re-layouts: 2.1 us -> 0.67 us
  transfers between devices with their start and end apart: 3 -> 1, of which waited for: 3 -> 1; matrix products, arithmetic and copies ran while one was open for 0% -> 1% of each run, Pallas kernels for 0% -> 2%
where the time goes in v2:
time: 67.9 us; the launch traced here: 67.4 us
  blocking collectives  42.5 us (63%)
  Pallas kernels  10.5 us (15%)
  starting transfers between devices  6.82 us (10%)
  waiting for transfers between devices  4.93 us (7%)
  between operations  1.33 us (2%)
  local copies, waits for them, and re-layouts  0.71 us (1%)
    all_gather x2, blocking collectives, beside(): return lax.all_gather(swapped, 'core')  14.3 us
    all_to_all x1, blocking collectives, to_row(): lax.all_to_all(jnp.broadcast_to(both[None], (chips,) + both.shape), 'chip...  12.3 us
    all_gather x2, blocking collectives, beside(): lax.all_gather(rows, ('state', 'chip', 'core'), axis_index_groups=groups)  10.2 us
    all_to_all x1, starting transfers between devices, local(): row = lax.all_gather(lax.all_to_all(sent, 'chip', 0, 0), 'core', axis=0)  6.82 us
    all_to_all x1, waiting for transfers between devices, local(): row = lax.all_gather(lax.all_to_all(sent, 'chip', 0, 0), 'core', axis=0)  4.93 us
    all_gather x1, blocking collectives, local(): row = lax.all_gather(lax.all_to_all(sent, 'chip', 0, 0), 'core', axis=0)  3.9 us
    pallas_call x1, Pallas kernels, local(): pl.pallas_call(first_kernel, out_shape=state_shapes + (jax.ShapeDtypeStru...  3.18 us
    pallas_call x1, Pallas kernels, local(): pl.pallas_call(second_kernel, out_shape=state_shapes, in_specs=[SMEM] + [...  2.91 us
  transfers between devices with their start and end apart: 1, of which 1 were waited for; matrix products, arithmetic and copies ran while one was open for 1% of the time, Pallas kernels for 2%

profile of v2, /device:TPU:7, one launch (start us, length us, event | category | flops | bytes accessed | tf_op | source)
XLA Modules:
  0.0 67.4 jit_solution(5146380333502488471)
XLA Ops:
  0.6 1.5 %pack.1 = bf16[8,2,32,128]{3,2,1,0:T(8,128)(2,1)} custom-call(bf16[2,32,80]{2,1,0:T(8,128)(2,1)} %bitcast.18, bf16[2,32]{1,0:T(2,128)(2,1)} %value_ref.1, bf16[2,32]{1,0:T(2,128)(2,1)} %var_ref.1), custom_call_target="tpu_custom_call" | custom-call | tf_op jit(solution)/shard_map/pack/pallas_call | solution.py:231
  2.2 6.8 %all-to-all-start.2 = ((bf16[8,2,32,128]{3,2,1,0:T(8,128)(2,1)}), bf16[8,2,32,128]{3,2,1,0:T(8,128)(2,1)S(1)}, u32[]{:S(2)}, u32[]{:S(2)}) async-start(bf16[8,2,32,128]{3,2,1,0:T(8,128)(2,1)} %pack.1), calls=%async_computation.2 | async-start | bytes 262144 | tf_op jit(solution)/shard_map/all_to_all | solution.py:238
  9.0 0.6 pad_add_fusion.place_ref
  9.6 1.6 %plan.1 = (s32[1,512]{1,0:T(1,128)S(1)}, s32[1,512]{1,0:T(1,128)}, s32[1]{0:T(128)}) custom-call(s32[4]{0:T(128)} %pad_add_fusion.place_ref, s32[1,512]{1,0:T(1,128)} %bitcast.19), custom_call_target="tpu_custom_call" | custom-call | tf_op jit(solution)/shard_map/plan/pallas_call | solution.py:241
  11.8 4.9 %all-to-all-done.2 = bf16[8,2,32,128]{3,2,1,0:T(8,128)(2,1)S(1)} async-done(((bf16[8,2,32,128]{3,2,1,0:T(8,128)(2,1)}), bf16[8,2,32,128]{3,2,1,0:T(8,128)(2,1)S(1)}, u32[]{:S(2)}, u32[]{:S(2)}) %all-to-all-start.2) | async-done | bytes 131104 | tf_op jit(solution)/shard_map/all_to_all | solution.py:238
  16.8 3.9 %all-gather.2 = bf16[16,2,32,128]{3,2,1,0:T(8,128)(2,1)S(1)} all-gather(bf16[8,2,32,128]{3,2,1,0:T(8,128)(2,1)S(1)} %all-to-all-done.2), channel_id=4, replica_groups=mesh['state'=32,'chip'=8,'core'=2] {'core'}, dimensions={0}, use_global_device_ids=true | all-gather | bytes 393216 | tf_op jit(solution)/shard_map/all_gather | solution.py:238
  20.7 5.6 %all-gather.3 = bf16[4,8,1,32,128]{4,3,2,1,0:T(8,128)(2,1)S(1)} all-gather(bf16[2,8,1,32,128]{4,3,2,1,0:T(8,128)(2,1)S(1)} %slice.24), channel_id=5, replica_groups={{1,16},{3,18},{5,20},{7,22},{9,24},{11,26},{13,28},{15,30},{17,32},{19,..., dimensions={0}, use_global_device_ids=true | all-gather | bytes 393216 | tf_op jit(solution)/shard_map/all_gather | solution.py:215
  26.3 0.0 copy-start.6
  26.3 9.0 %all-gather.4 = bf16[4,2,8,32,128]{4,3,2,1,0:T(8,128)(2,1)S(1)} all-gather(bf16[2,2,8,32,128]{4,3,2,1,0:T(8,128)(2,1)S(1)} %bitcast.16), channel_id=6, replica_groups=mesh['state'=32,'chip'=8,'core'=2] {'core'}, dimensions={0}, use_global_device_ids=true | all-gather | bytes 786432 | tf_op jit(solution)/shard_map/all_gather | solution.py:216
  35.4 0.0 copy-done
  35.4 0.0 copy-done.1
  35.4 0.0 copy-done.2
  35.4 0.0 copy-done.5
  35.4 0.0 copy-done.6
  35.4 0.6 copy-done.3
  36.1 0.0 copy-done.4
  36.1 3.2 %first.1 = (f32[2,1024]{1,0:T(2,128)S(1)}, bf16[2,80,1024]{2,1,0:T(8,128)(2,1)S(1)}, bf16[80,128]{1,0:T(8,128)(2,1)S(1)}, bf16[80,512]{1,0:T(8,128)(2,1)S(1)}, bf16[16,1536]{1,0:T(8,128)(2,1)S(1)}) custom-call(s32[4]{0:T(128)S(1)} %copy-done.4, bf16[2,8,2,32,128]{4,3,2,1,0:T(8,128)(2,1)S(1)} %bitcast.14, bf16[2,2,2,8,32,128]{5,4,3,2,1,0:T(8,128)(2,1)S(1)} %bitcast.12, ...), custom_call_target="tpu_custom_call" | custom-call | tf_op jit(solution)/shard_map/first/pallas_call | solution.py:255
  39.2 15.4 %conditional.1 = (bf16[80,512]{1,0:T(8,128)(2,1)S(1)}) conditional(s32[]{:T(128)} %bitcast.5, bf16[80,512]{1,0:T(8,128)(2,1)S(1)} %get-tuple-element.23, (bf16[80,128]{1,0:T(8,128)(2,1)S(1)}, s32[1,512]{1,0:T(1,128)S(1)}) %tuple.13), branch_computations={%region_0.0_spmd, %region_2.0_spmd} | conditional | flops 327680 | bytes 3276810 | solution.py:287
  39.3 1.9 %all-gather.1 = bf16[160,128]{1,0:T(8,128)(2,1)S(1)} all-gather(bf16[80,128]{1,0:T(8,128)(2,1)S(1)} %get-tuple-element.8), channel_id=3, replica_groups=mesh['state'=32,'chip'=8,'core'=2] {'core'}, dimensions={0}, use_global_device_ids=true | all-gather | bytes 61440 | tf_op jit(solution)/shard_map/cond/branch_1_fun/all_gather | solution.py:275
  41.2 12.3 %all_to_all.14.packed_ref = bf16[8,80,128]{2,1,0:T(8,128)(2,1)} all-to-all(bf16[8,80,128]{2,1,0:T(8,128)(2,1)S(1)} %broadcast_in_dim.12), channel_id=1, replica_groups=mesh['state'=32,'chip'=8,'core'=2] {'chip'}, dimensions={0} | all-to-all | bytes 327680 | tf_op jit(solution)/shard_map/cond/branch_1_fun/all_to_all | solution.py:277
  53.4 1.2 %spread.1 = bf16[80,512]{1,0:T(8,128)(2,1)S(1)} custom-call(bf16[8,80,128]{2,1,0:T(8,128)(2,1)} %all_to_all.14.packed_ref, s32[1,512]{1,0:T(1,128)S(1)} %get-tuple-element.9.slot_ref), custom_call_target="tpu_custom_call" | custom-call | tf_op jit(solution)/shard_map/cond/branch_1_fun/spread/pallas_call | solution.py:280
  54.7 4.5 %all-gather.5 = bf16[160,512]{1,0:T(8,128)(2,1)S(1)} all-gather(bf16[80,512]{1,0:T(8,128)(2,1)S(1)} %get-tuple-element.28.own_ref), channel_id=7, replica_groups={{1,16},{3,18},{5,20},{7,22},{9,24},{11,26},{13,28},{15,30},{17,32},{19,..., dimensions={0}, use_global_device_ids=true | all-gather | bytes 245760 | tf_op jit(solution)/shard_map/all_gather | solution.py:215
  59.2 5.3 %all-gather.6 = bf16[4,80,512]{2,1,0:T(8,128)(2,1)S(1)} all-gather(bf16[2,80,512]{2,1,0:T(8,128)(2,1)S(1)} %bitcast.17), channel_id=8, replica_groups=mesh['state'=32,'chip'=8,'core'=2] {'core'}, dimensions={0}, use_global_device_ids=true | all-gather | bytes 491520 | tf_op jit(solution)/shard_map/all_gather | solution.py:216
  64.5 2.9 %second.1 = (f32[2,1024]{1,0:T(2,128)}, bf16[2,80,1024]{2,1,0:T(8,128)(2,1)}) custom-call(s32[4]{0:T(128)S(1)} %copy-done.4, bf16[80,512]{1,0:T(8,128)(2,1)S(1)} %get-tuple-element.28.own_ref, bf16[2,2,80,512]{3,2,1,0:T(8,128)(2,1)S(1)} %bitcast.15, bf16[16,1536]{1,0:T(8,128)(2,1)S(1)} %get-tuple-element.25.errors_ref, s32[2,2,256]{2,1,0:T(2,128)S(1)} %copy-done.3, ...), custom_call_target="tpu_custom_call" | custom-call | tf_op jit(solution)/shard_map/second/pallas_call | solution.py:290
  (9 shorter events, 0.0 us)
Async XLA Ops:
  2.2 14.6 %all-to-all-start.2 = ((bf16[8,2,32,128]{3,2,1,0:T(8,128)(2,1)}), bf16[8,2,32,128]{3,2,1,0:T(8,128)(2,1)S(1)}, u32[]{:S(2)}, u32[]{:S(2)}) async-start(bf16[8,2,32,128]{3,2,1,0:T(8,128)(2,1)} %pack.1), calls=%async_computation.2 | async-start | bytes 262144 | tf_op jit(solution)/shard_map/all_to_all | solution.py:238
  26.3 9.1 %copy-start = (bf16[2,2,256,128]{3,2,1,0:T(8,128)(2,1)S(1)}, bf16[2,2,256,128]{3,2,1,0:T(8,128)(2,1)}, u32[]{:S(2)}) copy-start(bf16[2,2,256,128]{3,2,1,0:T(8,128)(2,1)} %taper_ref.3) | copy-start | bytes 786436
  26.3 9.1 %copy-start.1 = (bf16[2,80,1024]{2,1,0:T(8,128)(2,1)S(1)}, bf16[2,80,1024]{2,1,0:T(8,128)(2,1)}, u32[]{:S(2)}) copy-start(bf16[2,80,1024]{2,1,0:T(8,128)(2,1)} %anom_ref.1) | copy-start | bytes 983044
  26.3 9.1 %copy-start.2 = (f32[8,512]{1,0:T(8,128)S(1)}, f32[8,512]{1,0:T(8,128)}, u32[]{:S(2)}) copy-start(f32[8,512]{1,0:T(8,128)} %weight_ref.1) | copy-start | bytes 49156
  26.3 9.1 %copy-start.5 = (f32[2,1024]{1,0:T(2,128)S(1)}, f32[2,1024]{1,0:T(2,128)}, u32[]{:S(2)}) copy-start(f32[2,1024]{1,0:T(2,128)} %mean_ref.1) | copy-start | bytes 24580
  26.3 9.1 %copy-start.6 = (s32[1,512]{1,0:T(1,128)S(1)}, s32[1,512]{1,0:T(1,128)}, u32[]{:S(2)}) copy-start(s32[1,512]{1,0:T(1,128)} %get-tuple-element.21.home_ref) | copy-start | bytes 6148
  35.4 0.7 %copy-start.3 = (s32[2,2,256]{2,1,0:T(2,128)S(1)}, s32[2,2,256]{2,1,0:T(2,128)}, u32[]{:S(2)}) copy-start(s32[2,2,256]{2,1,0:T(2,128)} %lists_ref.3) | copy-start | bytes 12292
  35.4 0.7 %copy-start.4 = (s32[4]{0:T(128)S(1)}, s32[4]{0:T(128)}, u32[]{:S(2)}) copy-start(s32[4]{0:T(128)} %pad_add_fusion.place_ref) | copy-start | bytes 52

commit v3 on v2

--- a/solution.py
+++ b/solution.py
@@ -11,10 +11,12 @@
 F32 = jnp.float32
 BF16 = jnp.bfloat16
 LANES = 128
-SLOTS = 128
+SLOTS = 64
+SLOT, MINE, NEAR, LISTS = 0, 1, 2, 3
 VMEM = pl.BlockSpec(memory_space=pltpu.VMEM)
 SMEM = pl.BlockSpec(memory_space=pltpu.SMEM)
-PARAMS = pltpu.CompilerParams(vmem_limit_bytes=24 * 1024 * 1024)
+SMALL = pltpu.CompilerParams(vmem_limit_bytes=8 * 1024 * 1024)
+LARGE = pltpu.CompilerParams(vmem_limit_bytes=24 * 1024 * 1024)
 
 
 def dot(a, b, contract=((1,), (0,))):
@@ -33,7 +35,15 @@
     return one_hot(iota((size, size), 0) == iota((size, size), 1))
 
 
-def pack_kernel(prior_ref, value_ref, var_ref, rows_ref):
+def pack_kernel(prior_in, value_in, var_in, rows_ref, prior_ref, value_ref, var_ref, sems):
+    copies = [
+        pltpu.make_async_copy(source, target, sems.at[i])
+        for i, (source, target) in enumerate(((prior_in, prior_ref), (value_in, value_ref), (var_in, var_ref)))
+    ]
+    for copy in copies:
+        copy.start()
+    for copy in copies:
+        copy.wait()
     _, width, members = prior_ref.shape
     row = iota((LANES, width), 0) - members
     value = value_ref[...].astype(F32)
@@ -113,12 +123,14 @@
 
 
 def update_tiles(
-    listed, lists_ref, colour, base, members, value_row, mean_ref, anom_ref, taper_ref,
+    listed, table_ref, colour, members, value_row, mean_ref, anom_ref, taper_ref,
     new_mean_ref, new_anom_ref, scaled_ref, change_ref,
 ):
     bases = []
+    length = taper_ref.shape[2]
     for tile in range(anom_ref.shape[0]):
-        picked = pick(listed, lists_ref[colour, tile : tile + 1] - base)
+        ids = table_ref[LISTS + colour : LISTS + colour + 1, tile * length : (tile + 1) * length]
+        picked = pick(listed, ids)
         bases.append(
             scale_tile(
                 picked, members, value_row, mean_ref, anom_ref, taper_ref, colour, tile, new_mean_ref, scaled_ref
@@ -130,23 +142,34 @@
         )
 
 
-def plan_kernel(chips, chip_columns, place_ref, home_ref, slot_ref, near_ref, crowded_ref):
+def plan_kernel(chips, tile_columns, home_ref, lists_ref, table_ref, crowded_ref):
+    colours, tiles, length = lists_ref.shape
     region = home_ref.shape[1]
-    column = home_ref[...] - place_ref[2]
-    near_ref[...] = home_ref[...] - place_ref[1]
-    chip = jnp.zeros_like(column)
-    for edge in range(1, chips):
-        chip = chip + jnp.where(column >= edge * chip_columns, 1, 0)
-    chip = chip.astype(F32)
-    across = jnp.broadcast_to(chip, (8, region)).T[:, 0:1]
-    earlier = (across == chip) & (iota((region, region), 0) < iota((region, region), 1))
+    state, own_chip, core = lax.axis_index("state"), lax.axis_index("chip"), lax.axis_index("core")
+    device_columns = tiles * tile_columns
+    own = own_chip * 2 + core
+    column = home_ref[...] - state * (chips * 2 * device_columns)
+    device = jnp.zeros_like(column)
+    for edge in range(1, chips * 2):
+        device = device + jnp.where(column >= edge * device_columns, 1, 0)
+    device = device.astype(F32)
+    across = jnp.broadcast_to(device, (8, region)).T[:, 0:1]
+    earlier = (across == device) & (iota((region, region), 0) < iota((region, region), 1))
     rank = jnp.sum(jnp.where(earlier, 1.0, 0.0), axis=0, keepdims=True)
-    slot_ref[...] = (chip * SLOTS + rank).astype(jnp.int32)
+    slot = (device * SLOTS + rank).astype(jnp.int32)
+    table_ref[SLOT : SLOT + 1] = slot
+    table_ref[MINE : MINE + 1] = slot - own * SLOTS
+    table_ref[NEAR : NEAR + 1] = column - own * device_columns
+    for colour in range(colours):
+        for tile in range(tiles):
+            table_ref[LISTS + colour : LISTS + colour + 1, tile * length : (tile + 1) * length] = (
+                lists_ref[colour, tile : tile + 1] - (state - 1) * region
+            )
     crowded_ref[0] = (jnp.max(rank) >= SLOTS).astype(jnp.int32)
 
 
 def first_kernel(
-    place_ref, row_ref, beside_ref, lists_ref, home_ref, slot_ref, weight_ref, mean_ref, anom_ref, taper_ref,
+    row_ref, beside_ref, table_ref, weight_ref, mean_ref, anom_ref, taper_ref,
     new_mean_ref, new_anom_ref, packed_ref, prior_ref, errors_ref, rows_ref, scaled_ref, change_ref,
 ):
     members = anom_ref.shape[1]
@@ -156,19 +179,18 @@
         for core in range(2):
             at = (chip * 2 + core) * width
             for part, block in enumerate(
-                (beside_ref[0, 0, core, chip], row_ref[core, chip, 0], beside_ref[1, 1, core, chip], row_ref[core, chip, 1])
+                (beside_ref[0, core, chip], row_ref[core, chip, 0], beside_ref[1, core, chip], row_ref[core, chip, 1])
             ):
                 rows_ref[part * region + at : part * region + at + width] = block
     turn = identity(LANES)
     fields = dot(turn, rows_ref[...], ((1,), (1,)))
     listed = fields[: members + 16, : 3 * region].astype(BF16)
     errors_ref[...] = listed[members:]
-    base = place_ref[0] * region
     update_tiles(
-        listed, lists_ref, 0, base, members, members, mean_ref, anom_ref, taper_ref,
+        listed, table_ref, 0, members, members, mean_ref, anom_ref, taper_ref,
         new_mean_ref, new_anom_ref, scaled_ref, change_ref,
     )
-    home = home_ref[...]
+    home = table_ref[NEAR : NEAR + 1]
     columns = change_ref.shape[2]
     at_home = one_hot(iota((columns, region), 0) == home)
     prior = fields[:members, 3 * region :]
@@ -179,30 +201,38 @@
     inside = (home >= 0) & (home < columns)
     updated = jnp.where(inside, prior + increment, 0.0).astype(BF16)
     prior_ref[...] = updated
-    to_slot = one_hot(iota((SLOTS, region), 0) + place_ref[3] * SLOTS == slot_ref[...])
-    packed_ref[...] = dot(updated, to_slot, ((1,), (1,))).astype(BF16)
-
-
-def spread_kernel(packed_ref, slot_ref, prior_ref):
-    region = slot_ref.shape[1]
+    lane = iota((LANES, region), 0)
+    to_slot = one_hot(jnp.where(lane < SLOTS, lane, lane - SLOTS) == table_ref[MINE : MINE + 1])
+    twice = dot(updated, to_slot, ((1,), (1,)))
+    half = members // 2
+    packed_ref[...] = jnp.where(iota((half, LANES), 1) < SLOTS, twice[:half], twice[half:]).astype(BF16)
+
+
+def spread_kernel(packed_ref, table_ref, prior_ref):
+    region = table_ref.shape[1]
+    _, chips, half, _ = packed_ref.shape
+    first = iota((half, LANES), 1) < SLOTS
+    rows = iota((2 * SLOTS, region), 0)
     total = None
-    for chip in range(packed_ref.shape[0]):
-        from_slot = one_hot(iota((SLOTS, region), 0) + chip * SLOTS == slot_ref[...])
-        part = dot(packed_ref[chip], from_slot)
+    for chip in range(chips):
+        low, high = packed_ref[0, chip].astype(F32), packed_ref[1, chip].astype(F32)
+        upper = jnp.where(first, low, pltpu.roll(high, SLOTS, 1))
+        lower = jnp.where(first, pltpu.roll(low, SLOTS, 1), high)
+        ensemble = jnp.concatenate([upper, lower], axis=0).astype(BF16)
+        part = dot(ensemble, one_hot(rows + chip * 2 * SLOTS == table_ref[SLOT : SLOT + 1]))
         total = part if total is None else total + part
     prior_ref[...] = total.astype(BF16)
 
 
 def second_kernel(
-    place_ref, own_ref, beside_ref, errors_ref, lists_ref, mean_ref, anom_ref, taper_ref,
+    own_ref, beside_ref, errors_ref, table_ref, mean_ref, anom_ref, taper_ref,
     new_mean_ref, new_anom_ref, scaled_ref,
 ):
     members = anom_ref.shape[1]
-    ensemble = jnp.concatenate([beside_ref[0, 0], own_ref[...], beside_ref[1, 1]], axis=1)
+    ensemble = jnp.concatenate([beside_ref[0], own_ref[...], beside_ref[1]], axis=1)
     listed = jnp.concatenate([ensemble, errors_ref[...]], axis=0)
-    base = place_ref[0] * own_ref.shape[1]
     update_tiles(
-        listed, lists_ref, 1, base, members, members + 2, mean_ref, anom_ref, taper_ref,
+        listed, table_ref, 1, members, members + 2, mean_ref, anom_ref, taper_ref,
         new_mean_ref, new_anom_ref, scaled_ref, None,
     )
 
@@ -213,7 +243,8 @@
     for state, core in ((0, 0), (states - 1, 1)):
         groups += [[at(state, c, core), at(state, c + 1, core)] for c in range(0, chips, 2)]
     swapped = lax.all_gather(rows, ("state", "chip", "core"), axis_index_groups=groups)
-    return lax.all_gather(swapped, "core")
+    partner = lax.dynamic_index_in_dim(swapped, lax.axis_index("core"), axis=0, keepdims=False)
+    return lax.all_gather(partner, "core")
 
 
 def local(state_mean, state_anom, obs_prior, obs_value, obs_var, obs_weight, obs_home, tile_obs, taper):
@@ -222,29 +253,27 @@
     chips, states = lax.axis_size("chip"), lax.axis_size("state")
     width = obs_prior.shape[2]
     region = 2 * chips * width
-    state, chip, core = lax.axis_index("state"), lax.axis_index("chip"), lax.axis_index("core")
-    chip_columns = 2 * tiles * tile_width
-    row_column = state * chips * chip_columns
-    first_column = row_column + chip * chip_columns + core * tiles * tile_width
-    place = jnp.stack([state - 1, first_column, row_column, chip]).astype(jnp.int32)
-
+    raw = (jnp.swapaxes(obs_prior, 1, 2), obs_value, obs_var)
     sent = pl.pallas_call(
         pack_kernel,
-        out_shape=jax.ShapeDtypeStruct((chips, 2, width, LANES), BF16),
-        in_specs=[VMEM] * 3,
+        out_shape=pltpu.VMEM((chips, 2, width, LANES), BF16),
+        in_specs=[pl.BlockSpec(memory_space=pltpu.HBM)] * 3,
         out_specs=VMEM,
+        scratch_shapes=[pltpu.VMEM(a.shape, a.dtype) for a in raw] + [pltpu.SemaphoreType.DMA((3,))],
+        compiler_params=SMALL,
         name="pack",
-    )(jnp.swapaxes(obs_prior, 1, 2), obs_value, obs_var)
+    )(*[pltpu.with_memory_space_constraint(a, pltpu.HBM) for a in raw])
     row = lax.all_gather(lax.all_to_all(sent, "chip", 0, 0), "core", axis=0)
     near = beside(row[:, :, 0], chips, states)
 
-    slot, home, crowded = pl.pallas_call(
-        functools.partial(plan_kernel, chips, chip_columns),
-        out_shape=(jax.ShapeDtypeStruct((1, region), jnp.int32),) * 2 + (jax.ShapeDtypeStruct((1,), jnp.int32),),
-        in_specs=[SMEM, VMEM],
-        out_specs=(VMEM, VMEM, SMEM),
+    table, crowded = pl.pallas_call(
+        functools.partial(plan_kernel, chips, tile_width),
+        out_shape=(jax.ShapeDtypeStruct((8, region), jnp.int32), jax.ShapeDtypeStruct((1,), jnp.int32)),
+        in_specs=[VMEM] * 2,
+        out_specs=(VMEM, SMEM),
+        compiler_params=SMALL,
         name="plan",
-    )(place, obs_home[None])
+    )(obs_home[None], tile_obs)
 
     state_shapes = (
         jax.ShapeDtypeStruct(state_mean.shape, state_mean.dtype),
@@ -256,46 +285,50 @@
         first_kernel,
         out_shape=state_shapes
         + (
-            jax.ShapeDtypeStruct((members, SLOTS), BF16),
+            jax.ShapeDtypeStruct((members // 2, LANES), BF16),
             prior_shape,
             jax.ShapeDtypeStruct((16, 3 * region), BF16),
         ),
-        in_specs=[SMEM] + [VMEM] * 9,
+        in_specs=[VMEM] * 7,
         out_specs=(VMEM,) * 5,
         scratch_shapes=[
             pltpu.VMEM((4 * region, LANES), BF16),
             scaled,
             pltpu.VMEM((cells // tile_width, members, tiles * tile_width), BF16),
         ],
-        compiler_params=PARAMS,
+        compiler_params=LARGE,
         name="first",
-    )(place, row, near, tile_obs, home, slot, obs_weight, state_mean, state_anom, taper)
+    )(row, near, table, obs_weight, state_mean, state_anom, taper)
 
     def to_row(part):
-        both = lax.all_gather(part, "core", axis=0)
-        both = both[0] + both[1]
-        return lax.all_to_all(jnp.broadcast_to(both[None], (chips,) + both.shape), "chip", 0, 0)
-
-    def by_slot(packed, prior, slot):
+        return lax.all_to_all(jnp.broadcast_to(part[None], (chips,) + part.shape), "chip", 0, 0)
+
+    def by_slot(packed, prior, table):
         return pl.pallas_call(
-            spread_kernel, out_shape=prior_shape, in_specs=[VMEM] * 2, out_specs=VMEM, name="spread"
-        )(to_row(packed), slot)
-
-    def whole(packed, prior, slot):
-        return jnp.sum(to_row(prior), axis=0, dtype=BF16)
-
-    own = lax.cond(crowded[0] == 0, by_slot, whole, packed, prior, slot)
+            spread_kernel,
+            out_shape=prior_shape,
+            in_specs=[VMEM] * 2,
+            out_specs=VMEM,
+            compiler_params=SMALL,
+            name="spread",
+        )(lax.all_gather(to_row(packed), "core"), table)
+
+    def whole(packed, prior, table):
+        both = lax.all_gather(prior, "core")
+        return jnp.sum(to_row(both[0] + both[1]), axis=0, dtype=BF16)
+
+    own = lax.cond(crowded[0] == 0, by_slot, whole, packed, prior, table)
     sides = beside(own, chips, states)
 
     return pl.pallas_call(
         second_kernel,
         out_shape=state_shapes,
-        in_specs=[SMEM] + [VMEM] * 7,
+        in_specs=[VMEM] * 7,
         out_specs=(VMEM,) * 2,
         scratch_shapes=[scaled],
-        compiler_params=PARAMS,
+        compiler_params=LARGE,
         name="second",
-    )(place, own, sides, errors, tile_obs, new_mean, new_anom, taper)
+    )(own, sides, errors, table, new_mean, new_anom, taper)
 
 
 def solution(mesh):

time: 67.9 us -> 62.7 us (0.923)
  Pallas kernels: 10.5 us -> 7.87 us
  blocking collectives: 42.5 us -> 39.9 us
    all_to_all x1, blocking collectives: 12.3 us -> 9.67 us  [to_row(): lax.all_to_all(jnp.broadcast_to(part[None], (chips,) + part.shape), 'chip...]
    pallas_call x3, Pallas kernels: 6.04 us -> 4.82 us  [the longest x1 2.36 us: local(): pl.pallas_call(second_kernel, out_shape=state_shapes, in_specs=[VMEM] * 7...]
    pallas_call x1, Pallas kernels: 1.24 us -> 0.4 us  [by_slot(): pl.pallas_call(spread_kernel, out_shape=prior_shape, in_specs=[VMEM] * 2,...]
  transfers between devices with their start and end apart: 1 -> 1, of which waited for: 1 -> 1; matrix products, arithmetic and copies ran while one was open for 1% -> 0% of each run, Pallas kernels for 2% -> 1%
where the time goes in v3:
time: 62.7 us; the launch traced here: 62.3 us
  blocking collectives  39.9 us (64%)
  Pallas kernels  7.87 us (13%)
  starting transfers between devices  6.83 us (11%)
  waiting for transfers between devices  5.5 us (9%)
  between operations  1.36 us (2%)
  local copies, waits for them, and re-layouts  0.75 us (1%)
    all_gather x2, blocking collectives, beside(): return lax.all_gather(partner, 'core')  12.6 us
    all_gather x2, blocking collectives, beside(): lax.all_gather(rows, ('state', 'chip', 'core'), axis_index_groups=groups)  10.5 us
    all_to_all x1, blocking collectives, to_row(): lax.all_to_all(jnp.broadcast_to(part[None], (chips,) + part.shape), 'chip...  9.67 us
    all_to_all x1, starting transfers between devices, local(): row = lax.all_gather(lax.all_to_all(sent, 'chip', 0, 0), 'core', axis=0)  6.83 us
    all_to_all x1, waiting for transfers between devices, local(): row = lax.all_gather(lax.all_to_all(sent, 'chip', 0, 0), 'core', axis=0)  5.5 us
    all_gather x1, blocking collectives, local(): row = lax.all_gather(lax.all_to_all(sent, 'chip', 0, 0), 'core', axis=0)  3.9 us
    all_gather x1, blocking collectives, by_slot(): lax.all_gather(to_row(packed), 'core')  3.29 us
    pallas_call x1, Pallas kernels, local(): pl.pallas_call(first_kernel, out_shape=state_shapes + (jax.ShapeDtypeStru...  2.65 us
  transfers between devices with their start and end apart: 1, of which 1 were waited for; matrix products, arithmetic and copies ran while one was open for 0% of the time, Pallas kernels for 1%

profile of v3, /device:TPU:7, one launch (start us, length us, event | category | flops | bytes accessed | tf_op | source)
XLA Modules:
  0.0 62.3 jit_solution(17085884541848092808)
XLA Ops:
  0.6 1.5 %pack.1 = bf16[8,2,32,128]{3,2,1,0:T(8,128)(2,1)} custom-call(bf16[2,32,80]{2,1,0:T(8,128)(2,1)} %bitcast.13, bf16[2,32]{1,0:T(2,128)(2,1)} %value_in.1, bf16[2,32]{1,0:T(2,128)(2,1)} %var_in.1), custom_call_target="tpu_custom_call" | custom-call | tf_op jit(solution)/shard_map/pack/pallas_call | solution.py:257
  2.2 6.8 %all-to-all-start.2 = ((bf16[8,2,32,128]{3,2,1,0:T(8,128)(2,1)}), bf16[8,2,32,128]{3,2,1,0:T(8,128)(2,1)S(1)}, u32[]{:S(2)}, u32[]{:S(2)}) async-start(bf16[8,2,32,128]{3,2,1,0:T(8,128)(2,1)} %pack.1), calls=%async_computation.2 | async-start | bytes 262144 | tf_op jit(solution)/shard_map/all_to_all | solution.py:266
  9.0 0.0 copy-start.5
  9.0 0.7 %copy-done.4 = s32[2,2,256]{2,1,0:T(2,128)S(1)} copy-done((s32[2,2,256]{2,1,0:T(2,128)S(1)}, s32[2,2,256]{2,1,0:T(2,128)}, u32[]{:S(2)}) %copy-start.4) | copy-done | bytes 4120
  9.7 0.0 copy-done.5
  9.7 0.9 %plan.1 = (s32[8,512]{1,0:T(8,128)S(1)}, s32[1]{0:T(128)}) custom-call(s32[1,512]{1,0:T(1,128)S(1)} %bitcast.10, s32[2,2,256]{2,1,0:T(2,128)S(1)} %copy-done.4), custom_call_target="tpu_custom_call" | custom-call | tf_op jit(solution)/shard_map/plan/pallas_call | solution.py:269
  11.3 5.5 %all-to-all-done.2 = bf16[8,2,32,128]{3,2,1,0:T(8,128)(2,1)S(1)} async-done(((bf16[8,2,32,128]{3,2,1,0:T(8,128)(2,1)}), bf16[8,2,32,128]{3,2,1,0:T(8,128)(2,1)S(1)}, u32[]{:S(2)}, u32[]{:S(2)}) %all-to-all-start.2) | async-done | bytes 131104 | tf_op jit(solution)/shard_map/all_to_all | solution.py:266
  16.8 3.9 %all-gather.2 = bf16[16,2,32,128]{3,2,1,0:T(8,128)(2,1)S(1)} all-gather(bf16[8,2,32,128]{3,2,1,0:T(8,128)(2,1)S(1)} %all-to-all-done.2), channel_id=4, replica_groups=mesh['state'=32,'chip'=8,'core'=2] {'core'}, dimensions={0}, use_global_device_ids=true | all-gather | bytes 393216 | tf_op jit(solution)/shard_map/all_gather | solution.py:266
  20.7 5.6 %all-gather.3 = bf16[4,8,1,32,128]{4,3,2,1,0:T(8,128)(2,1)S(1)} all-gather(bf16[2,8,1,32,128]{4,3,2,1,0:T(8,128)(2,1)S(1)} %slice.14), channel_id=5, replica_groups={{1,16},{3,18},{5,20},{7,22},{9,24},{11,26},{13,28},{15,30},{17,32},{19,..., dimensions={0}, use_global_device_ids=true | all-gather | bytes 393216 | tf_op jit(solution)/shard_map/all_gather | solution.py:245
  26.4 0.0 copy-start
  26.4 0.0 copy-start.2
  26.4 0.0 copy-start.3
  26.4 8.8 %all_gather.38.beside_ref = bf16[2,2,8,32,128]{4,3,2,1,0:T(8,128)(2,1)S(1)} all-gather(bf16[1,2,8,32,128]{4,3,2,1,0:T(8,128)(2,1)S(1)} %constant_dynamic-slice_fusion.1), channel_id=1, replica_groups=mesh['state'=32,'chip'=8,'core'=2] {'core'}, dimensions={0}, use_global_device_ids=true | all-gather | bytes 393216 | tf_op jit(solution)/shard_map/all_gather | solution.py:247
  35.2 0.0 copy-done.1
  35.3 0.0 copy-done
  35.3 0.0 copy-done.2
  35.3 2.7 %first.1 = (f32[2,1024]{1,0:T(2,128)S(1)}, bf16[2,80,1024]{2,1,0:T(8,128)(2,1)S(1)}, bf16[40,128]{1,0:T(8,128)(2,1)S(1)}, bf16[80,512]{1,0:T(8,128)(2,1)S(1)}, bf16[16,1536]{1,0:T(8,128)(2,1)S(1)}) custom-call(bf16[2,8,2,32,128]{4,3,2,1,0:T(8,128)(2,1)S(1)} %bitcast.8, bf16[2,2,8,32,128]{4,3,2,1,0:T(8,128)(2,1)S(1)} %all_gather.38.beside_ref, ...), custom_call_target="tpu_custom_call" | custom-call | tf_op jit(solution)/shard_map/first/pallas_call | solution.py:284
  37.9 13.4 %conditional.1 = (bf16[80,512]{1,0:T(8,128)(2,1)S(1)}) conditional(s32[]{:T(128)} %bitcast.2, bf16[80,512]{1,0:T(8,128)(2,1)S(1)} %get-tuple-element.21, (bf16[40,128]{1,0:T(8,128)(2,1)S(1)}, s32[8,512]{1,0:T(8,128)S(1)}) %tuple.13), branch_computations={%region_0.2_spmd, %region_2.3_spmd} | conditional | flops 327680 | bytes 3276810 | solution.py:320
  38.0 9.7 %all_to_all.14 = bf16[8,40,128]{2,1,0:T(8,128)(2,1)S(1)} all-to-all(bf16[8,40,128]{2,1,0:T(8,128)(2,1)S(1)} %broadcast_in_dim.10), channel_id=1, replica_groups=mesh['state'=32,'chip'=8,'core'=2] {'chip'}, dimensions={0} | all-to-all | bytes 163840 | tf_op jit(solution)/shard_map/cond/branch_1_fun/all_to_all | solution.py:304
  47.6 3.3 %all-gather.1 = bf16[16,40,128]{2,1,0:T(8,128)(2,1)S(1)} all-gather(bf16[8,40,128]{2,1,0:T(8,128)(2,1)S(1)} %all_to_all.14), channel_id=3, replica_groups=mesh['state'=32,'chip'=8,'core'=2] {'core'}, dimensions={0}, use_global_device_ids=true | all-gather | bytes 245760 | tf_op jit(solution)/shard_map/cond/branch_1_fun/all_gather | solution.py:314
  50.9 0.4 spread.1
  51.3 4.8 %all-gather.4 = bf16[160,512]{1,0:T(8,128)(2,1)S(1)} all-gather(bf16[80,512]{1,0:T(8,128)(2,1)S(1)} %get-tuple-element.26.own_ref), channel_id=6, replica_groups={{1,16},{3,18},{5,20},{7,22},{9,24},{11,26},{13,28},{15,30},{17,32},{19,..., dimensions={0}, use_global_device_ids=true | all-gather | bytes 245760 | tf_op jit(solution)/shard_map/all_gather | solution.py:245
  56.2 3.7 %all_gather.41.beside_ref = bf16[2,80,512]{2,1,0:T(8,128)(2,1)S(1)} all-gather(bf16[1,80,512]{2,1,0:T(8,128)(2,1)S(1)} %constant_dynamic-slice_fusion), channel_id=1, replica_groups=mesh['state'=32,'chip'=8,'core'=2] {'core'}, dimensions={0}, use_global_device_ids=true | all-gather | bytes 245760 | tf_op jit(solution)/shard_map/all_gather | solution.py:247
  59.9 2.4 %second.1 = (f32[2,1024]{1,0:T(2,128)}, bf16[2,80,1024]{2,1,0:T(8,128)(2,1)}) custom-call(bf16[80,512]{1,0:T(8,128)(2,1)S(1)} %get-tuple-element.26.own_ref, bf16[2,80,512]{2,1,0:T(8,128)(2,1)S(1)} %all_gather.41.beside_ref, bf16[16,1536]{1,0:T(8,128)(2,1)S(1)} %get-tuple-element.23.errors_ref, s32[8,512]{1,0:T(8,128)S(1)} %get-tuple-element.20.table_ref, ...), custom_call_target="tpu_custom_call" | custom-call | tf_op jit(solution)/shard_map/second/pallas_call | solution.py:323
  (7 shorter events, 0.0 us)
Async XLA Ops:
  2.2 14.6 %all-to-all-start.2 = ((bf16[8,2,32,128]{3,2,1,0:T(8,128)(2,1)}), bf16[8,2,32,128]{3,2,1,0:T(8,128)(2,1)S(1)}, u32[]{:S(2)}, u32[]{:S(2)}) async-start(bf16[8,2,32,128]{3,2,1,0:T(8,128)(2,1)} %pack.1), calls=%async_computation.2 | async-start | bytes 262144 | tf_op jit(solution)/shard_map/all_to_all | solution.py:266
  9.0 0.7 %copy-start.4 = (s32[2,2,256]{2,1,0:T(2,128)S(1)}, s32[2,2,256]{2,1,0:T(2,128)}, u32[]{:S(2)}) copy-start(s32[2,2,256]{2,1,0:T(2,128)} %lists_ref.1) | copy-start | bytes 12292
  9.0 0.7 %copy-start.5 = (s32[512]{0:T(512)S(1)}, s32[512]{0:T(512)}, u32[]{:S(2)}) copy-start(s32[512]{0:T(512)} %param.17) | copy-start | bytes 6148
  26.4 8.9 %copy-start.1 = (bf16[2,80,1024]{2,1,0:T(8,128)(2,1)S(1)}, bf16[2,80,1024]{2,1,0:T(8,128)(2,1)}, u32[]{:S(2)}) copy-start(bf16[2,80,1024]{2,1,0:T(8,128)(2,1)} %anom_ref.1) | copy-start | bytes 983044
  26.4 8.9 %copy-start = (bf16[2,2,256,128]{3,2,1,0:T(8,128)(2,1)S(1)}, bf16[2,2,256,128]{3,2,1,0:T(8,128)(2,1)}, u32[]{:S(2)}) copy-start(bf16[2,2,256,128]{3,2,1,0:T(8,128)(2,1)} %taper_ref.3) | copy-start | bytes 786436
  26.4 8.9 %copy-start.2 = (f32[8,512]{1,0:T(8,128)S(1)}, f32[8,512]{1,0:T(8,128)}, u32[]{:S(2)}) copy-start(f32[8,512]{1,0:T(8,128)} %weight_ref.1) | copy-start | bytes 49156
  26.4 8.9 %copy-start.3 = (f32[2,1024]{1,0:T(2,128)S(1)}, f32[2,1024]{1,0:T(2,128)}, u32[]{:S(2)}) copy-start(f32[2,1024]{1,0:T(2,128)} %mean_ref.1) | copy-start | bytes 24580

commit v4 on v3

--- a/solution.py
+++ b/solution.py
@@ -33,31 +33,6 @@
 
 def identity(size):
     return one_hot(iota((size, size), 0) == iota((size, size), 1))
-
-
-def pack_kernel(prior_in, value_in, var_in, rows_ref, prior_ref, value_ref, var_ref, sems):
-    copies = [
-        pltpu.make_async_copy(source, target, sems.at[i])
-        for i, (source, target) in enumerate(((prior_in, prior_ref), (value_in, value_ref), (var_in, var_ref)))
-    ]
-    for copy in copies:
-        copy.start()
-    for copy in copies:
-        copy.wait()
-    _, width, members = prior_ref.shape
-    row = iota((LANES, width), 0) - members
-    value = value_ref[...].astype(F32)
-    var = var_ref[...].astype(F32)
-    tail = jnp.where(row == 0, value[0:1], 0.0)
-    tail = jnp.where(row == 1, var[0:1], tail)
-    tail = jnp.where(row == 2, value[1:2], tail)
-    tail = jnp.where(row == 3, var[1:2], tail).astype(BF16)
-    spread = one_hot(iota((members, LANES), 0) == iota((members, LANES), 1))
-    first = dot(prior_ref[0], spread) + dot(identity(width), tail, ((1,), (1,)))
-    second = dot(prior_ref[1], spread)
-    for copy in range(rows_ref.shape[0]):
-        rows_ref[copy, 0] = first.astype(BF16)
-        rows_ref[copy, 1] = second.astype(BF16)
 
 
 def pick(fields, ids):
@@ -142,7 +117,34 @@
         )
 
 
-def plan_kernel(chips, tile_columns, home_ref, lists_ref, table_ref, crowded_ref):
+def prepare_kernel(
+    chips, tile_columns, prior_in, value_in, var_in, home_in, lists_in, mean_in,
+    first_ref, second_ref, table_ref, mean_ref, crowded_ref, prior_ref, value_ref, var_ref, home_ref, lists_ref, sems,
+):
+    copies = [
+        pltpu.make_async_copy(source, target, sems.at[i])
+        for i, (source, target) in enumerate(
+            (
+                (prior_in, prior_ref), (value_in, value_ref), (var_in, var_ref), (home_in, home_ref), (lists_in, lists_ref),
+                (mean_in, mean_ref),
+            )
+        )
+    ]
+    for copy in copies:
+        copy.start()
+    for copy in copies:
+        copy.wait()
+    _, width, members = prior_ref.shape
+    row = iota((LANES, width), 0) - members
+    value = value_ref[...].astype(F32)
+    var = var_ref[...].astype(F32)
+    tail = jnp.where(row == 0, value[0:1], 0.0)
+    tail = jnp.where(row == 1, var[0:1], tail)
+    tail = jnp.where(row == 2, value[1:2], tail)
+    tail = jnp.where(row == 3, var[1:2], tail).astype(BF16)
+    widen = one_hot(iota((members, LANES), 0) == iota((members, LANES), 1))
+    first_ref[...] = (dot(prior_ref[0], widen) + dot(identity(width), tail, ((1,), (1,)))).astype(BF16)
+    second_ref[...] = dot(prior_ref[1], widen).astype(BF16)
     colours, tiles, length = lists_ref.shape
     region = home_ref.shape[1]
     state, own_chip, core = lax.axis_index("state"), lax.axis_index("chip"), lax.axis_index("core")
@@ -169,17 +171,22 @@
 
 
 def first_kernel(
-    row_ref, beside_ref, table_ref, weight_ref, mean_ref, anom_ref, taper_ref,
+    records_ref, table_ref, weight_ref, mean_ref, anom_ref, taper_ref,
     new_mean_ref, new_anom_ref, packed_ref, prior_ref, errors_ref, rows_ref, scaled_ref, change_ref,
 ):
     members = anom_ref.shape[1]
-    _, chips, _, width, _ = row_ref.shape
+    _, dealt, _, width, _ = records_ref.shape
+    chips = dealt // 2
     region = 2 * chips * width
     for chip in range(chips):
         for core in range(2):
             at = (chip * 2 + core) * width
+            here = chip + (1 - core) * chips
             for part, block in enumerate(
-                (beside_ref[0, core, chip], row_ref[core, chip, 0], beside_ref[1, core, chip], row_ref[core, chip, 1])
+                (
+                    records_ref[0, chip, core], records_ref[core, here, 0],
+                    records_ref[1, chips + chip, core], records_ref[core, here, 1],
+                )
             ):
                 rows_ref[part * region + at : part * region + at + width] = block
     turn = identity(LANES)
@@ -243,8 +250,21 @@
     for state, core in ((0, 0), (states - 1, 1)):
         groups += [[at(state, c, core), at(state, c + 1, core)] for c in range(0, chips, 2)]
     swapped = lax.all_gather(rows, ("state", "chip", "core"), axis_index_groups=groups)
-    partner = lax.dynamic_index_in_dim(swapped, lax.axis_index("core"), axis=0, keepdims=False)
+    partner = jnp.where(lax.axis_index("core") == 1, swapped[1], swapped[0])
     return lax.all_gather(partner, "core")
+
+
+def across_two(first, second, crowded, chips, states):
+    at = lambda state, chip, core: (state * chips + chip) * 2 + core
+    groups = [
+        [at(s, c, 1) for c in range(chips)] + [at((s + 1) % states, c, 0) for c in range(chips)] for s in range(states)
+    ]
+    pair = lax.all_gather(first, "core")
+    own = jnp.stack([first, second])
+    low = (lax.iota(jnp.int32, 2 * chips) < chips) == (lax.axis_index("core") == 1)
+    sent = jnp.where(low[:, None, None, None], own[None], pair[None])
+    dealt = lax.all_to_all(sent, ("state", "chip", "core"), 0, 0, axis_index_groups=groups)
+    return lax.optimization_barrier((lax.all_gather(dealt, "core"), crowded))
 
 
 def local(state_mean, state_anom, obs_prior, obs_value, obs_var, obs_weight, obs_home, tile_obs, taper):
@@ -253,27 +273,24 @@
     chips, states = lax.axis_size("chip"), lax.axis_size("state")
     width = obs_prior.shape[2]
     region = 2 * chips * width
-    raw = (jnp.swapaxes(obs_prior, 1, 2), obs_value, obs_var)
-    sent = pl.pallas_call(
-        pack_kernel,
-        out_shape=pltpu.VMEM((chips, 2, width, LANES), BF16),
-        in_specs=[pl.BlockSpec(memory_space=pltpu.HBM)] * 3,
-        out_specs=VMEM,
-        scratch_shapes=[pltpu.VMEM(a.shape, a.dtype) for a in raw] + [pltpu.SemaphoreType.DMA((3,))],
+    raw = (jnp.swapaxes(obs_prior, 1, 2), obs_value, obs_var, obs_home[None], tile_obs, state_mean)
+    block = jax.ShapeDtypeStruct((width, LANES), BF16)
+    first, second, table, mean, crowded = pl.pallas_call(
+        functools.partial(prepare_kernel, chips, tile_width),
+        out_shape=(
+            block,
+            block,
+            jax.ShapeDtypeStruct((8, region), jnp.int32),
+            jax.ShapeDtypeStruct(state_mean.shape, state_mean.dtype),
+            pltpu.SMEM((1,), jnp.int32),
+        ),
+        in_specs=[pl.BlockSpec(memory_space=pltpu.HBM)] * len(raw),
+        out_specs=(VMEM, VMEM, VMEM, VMEM, SMEM),
+        scratch_shapes=[pltpu.VMEM(a.shape, a.dtype) for a in raw[:-1]] + [pltpu.SemaphoreType.DMA((len(raw),))],
         compiler_params=SMALL,
-        name="pack",
+        name="prepare",
     )(*[pltpu.with_memory_space_constraint(a, pltpu.HBM) for a in raw])
-    row = lax.all_gather(lax.all_to_all(sent, "chip", 0, 0), "core", axis=0)
-    near = beside(row[:, :, 0], chips, states)
-
-    table, crowded = pl.pallas_call(
-        functools.partial(plan_kernel, chips, tile_width),
-        out_shape=(jax.ShapeDtypeStruct((8, region), jnp.int32), jax.ShapeDtypeStruct((1,), jnp.int32)),
-        in_specs=[VMEM] * 2,
-        out_specs=(VMEM, SMEM),
-        compiler_params=SMALL,
-        name="plan",
-    )(obs_home[None], tile_obs)
+    records, crowded = across_two(first, second, crowded, chips, states)
 
     state_shapes = (
         jax.ShapeDtypeStruct(state_mean.shape, state_mean.dtype),
@@ -289,7 +306,7 @@
             prior_shape,
             jax.ShapeDtypeStruct((16, 3 * region), BF16),
         ),
-        in_specs=[VMEM] * 7,
+        in_specs=[VMEM] * 6,
         out_specs=(VMEM,) * 5,
         scratch_shapes=[
             pltpu.VMEM((4 * region, LANES), BF16),
@@ -298,7 +315,7 @@
         ],
         compiler_params=LARGE,
         name="first",
-    )(row, near, table, obs_weight, state_mean, state_anom, taper)
+    )(records, table, obs_weight, mean, state_anom, taper)
 
     def to_row(part):
         return lax.all_to_all(jnp.broadcast_to(part[None], (chips,) + part.shape), "chip", 0, 0)

time: 62.7 us -> 60.3 us (0.962)
  the two profiles are of different devices: /device:TPU:7 before, /device:TPU:1 now
where the time goes in v4:
time: 60.3 us; the launch traced here: 60 us
  blocking collectives  52.5 us (87%)
  Pallas kernels  6.64 us (11%)
  between operations  0.68 us (1%)
    all_to_all x1, blocking collectives, across_two(): lax.all_to_all(sent, ('state', 'chip', 'core'), 0, 0, axis_index_groups=g...  13.8 us
    all_to_all x1, blocking collectives, to_row(): lax.all_to_all(jnp.broadcast_to(part[None], (chips,) + part.shape), 'chip...  11.1 us
    all_gather x1, blocking collectives, across_two(): return lax.optimization_barrier((lax.all_gather(dealt, 'core'), crowded))  8.68 us
    all_gather x1, blocking collectives, across_two(): pair = lax.all_gather(first, 'core')  8.37 us
    all_gather x1, blocking collectives, beside(): lax.all_gather(rows, ('state', 'chip', 'core'), axis_index_groups=groups)  4.84 us
    all_gather x1, blocking collectives, by_slot(): lax.all_gather(to_row(packed), 'core')  3.46 us
    pallas_call x1, Pallas kernels, local(): pl.pallas_call(first_kernel, out_shape=state_shapes + (jax.ShapeDtypeStru...  2.65 us
    pallas_call x1, Pallas kernels, local(): pl.pallas_call(second_kernel, out_shape=state_shapes, in_specs=[VMEM] * 7...  2.35 us

profile of v4, /device:TPU:1, one launch (start us, length us, event | category | flops | bytes accessed | tf_op | source)
XLA Modules:
  0.0 60.0 jit_solution(17649085982592623995)
XLA Ops:
  0.6 1.2 %prepare.1 = (bf16[32,128]{1,0:T(8,128)(2,1)S(1)}, bf16[32,128]{1,0:T(8,128)(2,1)S(1)}, s32[8,512]{1,0:T(8,128)S(1)}, f32[2,1024]{1,0:T(2,128)S(1)}, s32[1]{0:T(128)S(4)}) custom-call(bf16[2,32,80]{2,1,0:T(8,128)(2,1)} %bitcast.15, bf16[2,32]{1,0:T(2,128)(2,1)} %value_in.1, bf16[2,32]{1,0:T(2,128)(2,1)} %var_in.1, s32[1,512]{1,0:T(1,128)} %bitcast.16, ...), custom_call_target="tpu_custom_call" | custom-call | tf_op jit(solution)/shard_map/prepare/pallas_call | solution.py:278
  1.9 8.4 %all-gather.2 = bf16[64,128]{1,0:T(8,128)(2,1)S(1)} all-gather(bf16[32,128]{1,0:T(8,128)(2,1)S(1)} %get-tuple-element.24), channel_id=4, replica_groups=mesh['state'=32,'chip'=8,'core'=2] {'core'}, dimensions={0}, use_global_device_ids=true | all-gather | bytes 24576 | tf_op jit(solution)/shard_map/all_gather | solution.py:262
  10.3 0.1 broadcast_select_fusion
  10.4 13.8 %all_to_all.15 = bf16[16,2,32,128]{3,2,1,0:T(8,128)(2,1)S(1)} all-to-all(bf16[16,2,32,128]{3,2,1,0:T(8,128)(2,1)S(1)} %broadcast_select_fusion), channel_id=1, replica_groups={{1,3,5,7,9,11,13,15,16,18,20,22,24,26,28,30},{17,19,21,23,25,27,29,31,3..., dimensions={0} | all-to-all | bytes 524288 | tf_op jit(solution)/shard_map/all_to_all | solution.py:266
  24.2 0.0 copy-start
  24.2 0.0 copy-start.1
  24.2 0.0 copy-start.2
  24.2 8.7 %all-gather.3 = bf16[32,2,32,128]{3,2,1,0:T(8,128)(2,1)S(1)} all-gather(bf16[16,2,32,128]{3,2,1,0:T(8,128)(2,1)S(1)} %all_to_all.15), channel_id=5, replica_groups=mesh['state'=32,'chip'=8,'core'=2] {'core'}, dimensions={0}, use_global_device_ids=true | all-gather | bytes 786432 | tf_op jit(solution)/shard_map/all_gather | solution.py:267
  32.9 0.0 copy-done
  32.9 0.0 copy-done.1
  32.9 0.0 copy-done.2
  32.9 2.6 %first.1 = (f32[2,1024]{1,0:T(2,128)S(1)}, bf16[2,80,1024]{2,1,0:T(8,128)(2,1)S(1)}, bf16[40,128]{1,0:T(8,128)(2,1)S(1)}, bf16[80,512]{1,0:T(8,128)(2,1)S(1)}, bf16[16,1536]{1,0:T(8,128)(2,1)S(1)}) custom-call(bf16[2,16,2,32,128]{4,3,2,1,0:T(8,128)(2,1)S(1)} %bitcast.9, s32[8,512]{1,0:T(8,128)S(1)} %get-tuple-element.29.table_ref, f32[8,512]{1,0:T(8,128)S(1)} %copy-done.2, ...), custom_call_target="tpu_custom_call" | custom-call | tf_op jit(solution)/shard_map/first/pallas_call | solution.py:301
  35.6 15.0 %conditional.1 = (bf16[80,512]{1,0:T(8,128)(2,1)S(1)}) conditional(s32[]{:T(128)} %bitcast.7, bf16[80,512]{1,0:T(8,128)(2,1)S(1)} %get-tuple-element.31, (bf16[40,128]{1,0:T(8,128)(2,1)S(1)}, s32[8,512]{1,0:T(8,128)S(1)}) %tuple.15), branch_computations={%region_0.2_spmd, %region_2.3_spmd} | conditional | flops 327680 | bytes 3276810 | solution.py:337
  35.6 11.1 %all_to_all.14 = bf16[8,40,128]{2,1,0:T(8,128)(2,1)S(1)} all-to-all(bf16[8,40,128]{2,1,0:T(8,128)(2,1)S(1)} %broadcast_in_dim.31), channel_id=1, replica_groups=mesh['state'=32,'chip'=8,'core'=2] {'chip'}, dimensions={0} | all-to-all | bytes 163840 | tf_op jit(solution)/shard_map/cond/branch_1_fun/all_to_all | solution.py:321
  46.7 3.5 %all-gather.1 = bf16[16,40,128]{2,1,0:T(8,128)(2,1)S(1)} all-gather(bf16[8,40,128]{2,1,0:T(8,128)(2,1)S(1)} %all_to_all.14), channel_id=3, replica_groups=mesh['state'=32,'chip'=8,'core'=2] {'core'}, dimensions={0}, use_global_device_ids=true | all-gather | bytes 245760 | tf_op jit(solution)/shard_map/cond/branch_1_fun/all_gather | solution.py:331
  50.2 0.4 spread.1
  50.6 4.8 %all-gather.4 = bf16[160,512]{1,0:T(8,128)(2,1)S(1)} all-gather(bf16[80,512]{1,0:T(8,128)(2,1)S(1)} %get-tuple-element.36.own_ref), channel_id=6, replica_groups={{1,16},{3,18},{5,20},{7,22},{9,24},{11,26},{13,28},{15,30},{17,32},{19,..., dimensions={0}, use_global_device_ids=true | all-gather | bytes 245760 | tf_op jit(solution)/shard_map/all_gather | solution.py:252
  55.4 2.2 %all-gather.5 = bf16[160,512]{1,0:T(8,128)(2,1)S(1)} all-gather(bf16[80,512]{1,0:T(8,128)(2,1)S(1)} %slice_select_fusion), channel_id=7, replica_groups=mesh['state'=32,'chip'=8,'core'=2] {'core'}, dimensions={0}, use_global_device_ids=true | all-gather | bytes 245760 | tf_op jit(solution)/shard_map/all_gather | solution.py:254
  57.6 2.4 %second.1 = (f32[2,1024]{1,0:T(2,128)}, bf16[2,80,1024]{2,1,0:T(8,128)(2,1)}) custom-call(bf16[80,512]{1,0:T(8,128)(2,1)S(1)} %get-tuple-element.36.own_ref, bf16[2,80,512]{2,1,0:T(8,128)(2,1)S(1)} %bitcast.10, bf16[16,1536]{1,0:T(8,128)(2,1)S(1)} %get-tuple-element.33.errors_ref, s32[8,512]{1,0:T(8,128)S(1)} %get-tuple-element.29.table_ref, ...), custom_call_target="tpu_custom_call" | custom-call | tf_op jit(solution)/shard_map/second/pallas_call | solution.py:340
  (4 shorter events, 0.0 us)
Async XLA Ops:
  24.2 8.7 %copy-start = (bf16[2,2,256,128]{3,2,1,0:T(8,128)(2,1)S(1)}, bf16[2,2,256,128]{3,2,1,0:T(8,128)(2,1)}, u32[]{:S(2)}) copy-start(bf16[2,2,256,128]{3,2,1,0:T(8,128)(2,1)} %taper_ref.3) | copy-start | bytes 786436
  24.2 8.7 %copy-start.1 = (bf16[2,80,1024]{2,1,0:T(8,128)(2,1)S(1)}, bf16[2,80,1024]{2,1,0:T(8,128)(2,1)}, u32[]{:S(2)}) copy-start(bf16[2,80,1024]{2,1,0:T(8,128)(2,1)} %anom_ref.1) | copy-start | bytes 983044
  24.2 8.7 %copy-start.2 = (f32[8,512]{1,0:T(8,128)S(1)}, f32[8,512]{1,0:T(8,128)}, u32[]{:S(2)}) copy-start(f32[8,512]{1,0:T(8,128)} %weight_ref.1) | copy-start | bytes 49156

commit v5 on v4

--- a/solution.py
+++ b/solution.py
@@ -12,6 +12,7 @@
 BF16 = jnp.bfloat16
 LANES = 128
 SLOTS = 64
+KEPT = 84
 SLOT, MINE, NEAR, LISTS = 0, 1, 2, 3
 VMEM = pl.BlockSpec(memory_space=pltpu.VMEM)
 SMEM = pl.BlockSpec(memory_space=pltpu.SMEM)
@@ -58,14 +59,8 @@
     return anomaly, coef_anom, coef_mean
 
 
-def scale_tile(picked, members, value_row, mean_ref, anom_ref, taper_ref, colour, tile, new_mean_ref, scaled_ref):
-    value = picked[value_row : value_row + 1]
-    var = picked[value_row + 1 : value_row + 2]
-    anomaly, coef_anom, coef_mean = package(picked[:members], value, var)
-    basis = anomaly.astype(BF16)
-    listed = basis.shape[1]
-    coefs = jnp.concatenate([coef_anom, coef_mean, jnp.zeros((6, listed), F32)], axis=0).T
-    taper = taper_ref[colour, tile].astype(F32)
+def scale_tile(basis, coefs, mean_ref, anom_ref, taper, tile, new_mean_ref, scaled_ref):
+    taper = taper.astype(F32)
     taper_anom = taper * coefs[:, 0:1]
     taper_mean = taper * coefs[:, 1:2]
     width = taper.shape[1]
@@ -78,7 +73,6 @@
             scaled_ref[tile, :, cells] = (taper_anom * level).astype(BF16)
             shift = jnp.sum(taper_mean * level, axis=0, keepdims=True)
             new_mean_ref[tile : tile + 1, cells] = mean_ref[tile : tile + 1, cells] + shift
-    return basis
 
 
 def shift_tile(basis, mean_ref, anom_ref, tile, new_mean_ref, new_anom_ref, scaled_ref, width, change_ref):
@@ -101,25 +95,46 @@
     listed, table_ref, colour, members, value_row, mean_ref, anom_ref, taper_ref,
     new_mean_ref, new_anom_ref, scaled_ref, change_ref,
 ):
-    bases = []
-    length = taper_ref.shape[2]
-    for tile in range(anom_ref.shape[0]):
-        ids = table_ref[LISTS + colour : LISTS + colour + 1, tile * length : (tile + 1) * length]
-        picked = pick(listed, ids)
-        bases.append(
-            scale_tile(
-                picked, members, value_row, mean_ref, anom_ref, taper_ref, colour, tile, new_mean_ref, scaled_ref
-            )
+    tiles, length = taper_ref.shape[1], taper_ref.shape[2]
+    picked = pick(listed, table_ref[LISTS + colour : LISTS + colour + 1])
+    anomaly, coef_anom, coef_mean = package(
+        picked[:members], picked[value_row : value_row + 1], picked[value_row + 1 : value_row + 2]
+    )
+    basis = anomaly.astype(BF16)
+    coefs = jnp.concatenate([coef_anom, coef_mean, jnp.zeros((6, tiles * length), F32)], axis=0).T
+    for tile in range(tiles):
+        own = slice(tile * length, (tile + 1) * length)
+        scale_tile(
+            basis[:, own], coefs[own], mean_ref, anom_ref, taper_ref[colour, tile], tile, new_mean_ref, scaled_ref
         )
-    for tile, basis in enumerate(bases):
+    for tile in range(tiles):
+        own = slice(tile * length, (tile + 1) * length)
         shift_tile(
-            basis, mean_ref, anom_ref, tile, new_mean_ref, new_anom_ref, scaled_ref, taper_ref.shape[3], change_ref
+            basis[:, own], mean_ref, anom_ref, tile, new_mean_ref, new_anom_ref, scaled_ref, taper_ref.shape[3],
+            change_ref,
         )
+
+
+def fold(block, other):
+    other = pltpu.roll(other, KEPT, 1)
+    lane = iota(block.shape, 1)
+    half = block.shape[0] // 2
+    beneath = jnp.where(lane[:half] < LANES // 2, other[:half], pltpu.roll(other[half:], LANES // 2, 1))
+    return jnp.concatenate([jnp.where(lane < KEPT, block, other), beneath], axis=0).astype(BF16)
+
+
+def unfold(folded):
+    folded = folded.astype(F32)
+    width = folded.shape[0] * 2 // 3
+    beneath = folded[width:]
+    other = jnp.concatenate([beneath, pltpu.roll(beneath, LANES // 2, 1)], axis=0)
+    lane = iota((width, LANES), 1)
+    return pltpu.roll(jnp.where(lane < KEPT, other, folded[:width]), LANES - KEPT, 1).astype(BF16)
 
 
 def prepare_kernel(
     chips, tile_columns, prior_in, value_in, var_in, home_in, lists_in, mean_in,
-    first_ref, second_ref, table_ref, mean_ref, crowded_ref, prior_ref, value_ref, var_ref, home_ref, lists_ref, sems,
+    own_ref, pair_ref, table_ref, mean_ref, crowded_ref, prior_ref, value_ref, var_ref, home_ref, lists_ref, sems,
 ):
     copies = [
         pltpu.make_async_copy(source, target, sems.at[i])
@@ -143,8 +158,12 @@
     tail = jnp.where(row == 2, value[1:2], tail)
     tail = jnp.where(row == 3, var[1:2], tail).astype(BF16)
     widen = one_hot(iota((members, LANES), 0) == iota((members, LANES), 1))
-    first_ref[...] = (dot(prior_ref[0], widen) + dot(identity(width), tail, ((1,), (1,)))).astype(BF16)
-    second_ref[...] = dot(prior_ref[1], widen).astype(BF16)
+    first = dot(prior_ref[0], widen) + dot(identity(width), tail, ((1,), (1,)))
+    second = dot(prior_ref[1], widen)
+    none = jnp.zeros_like(first)
+    on_first = lax.axis_index("core") == 0
+    own_ref[...] = fold(first, second)
+    pair_ref[...] = fold(jnp.where(on_first, first, none), jnp.where(on_first, none, first))
     colours, tiles, length = lists_ref.shape
     region = home_ref.shape[1]
     state, own_chip, core = lax.axis_index("state"), lax.axis_index("chip"), lax.axis_index("core")
@@ -175,20 +194,20 @@
     new_mean_ref, new_anom_ref, packed_ref, prior_ref, errors_ref, rows_ref, scaled_ref, change_ref,
 ):
     members = anom_ref.shape[1]
-    _, dealt, _, width, _ = records_ref.shape
-    chips = dealt // 2
+    _, dealt, height, _ = records_ref.shape
+    chips, width = dealt // 2, height * 2 // 3
     region = 2 * chips * width
     for chip in range(chips):
+        at = chip * 2 * width
+        for side, part in ((0, 0), (1, 2)):
+            folded = records_ref[side, side * chips + chip]
+            rows_ref[part * region + at : part * region + at + width] = folded[:width]
+            rows_ref[part * region + at + width : part * region + at + 2 * width] = unfold(folded)
         for core in range(2):
-            at = (chip * 2 + core) * width
-            here = chip + (1 - core) * chips
-            for part, block in enumerate(
-                (
-                    records_ref[0, chip, core], records_ref[core, here, 0],
-                    records_ref[1, chips + chip, core], records_ref[core, here, 1],
-                )
-            ):
-                rows_ref[part * region + at : part * region + at + width] = block
+            folded = records_ref[core, chip + (1 - core) * chips]
+            here = at + core * width
+            rows_ref[region + here : region + here + width] = folded[:width]
+            rows_ref[3 * region + here : 3 * region + here + width] = unfold(folded)
     turn = identity(LANES)
     fields = dot(turn, rows_ref[...], ((1,), (1,)))
     listed = fields[: members + 16, : 3 * region].astype(BF16)
@@ -254,15 +273,14 @@
     return lax.all_gather(partner, "core")
 
 
-def across_two(first, second, crowded, chips, states):
+def across_two(own, pair, crowded, chips, states):
     at = lambda state, chip, core: (state * chips + chip) * 2 + core
     groups = [
         [at(s, c, 1) for c in range(chips)] + [at((s + 1) % states, c, 0) for c in range(chips)] for s in range(states)
     ]
-    pair = lax.all_gather(first, "core")
-    own = jnp.stack([first, second])
+    pair = lax.all_gather(pair, "core")
     low = (lax.iota(jnp.int32, 2 * chips) < chips) == (lax.axis_index("core") == 1)
-    sent = jnp.where(low[:, None, None, None], own[None], pair[None])
+    sent = jnp.where(low[:, None, None], own[None], (pair[0] + pair[1])[None])
     dealt = lax.all_to_all(sent, ("state", "chip", "core"), 0, 0, axis_index_groups=groups)
     return lax.optimization_barrier((lax.all_gather(dealt, "core"), crowded))
 
@@ -274,8 +292,8 @@
     width = obs_prior.shape[2]
     region = 2 * chips * width
     raw = (jnp.swapaxes(obs_prior, 1, 2), obs_value, obs_var, obs_home[None], tile_obs, state_mean)
-    block = jax.ShapeDtypeStruct((width, LANES), BF16)
-    first, second, table, mean, crowded = pl.pallas_call(
+    block = jax.ShapeDtypeStruct((width * 3 // 2, LANES), BF16)
+    own, pair, table, mean, crowded = pl.pallas_call(
         functools.partial(prepare_kernel, chips, tile_width),
         out_shape=(
             block,
@@ -290,7 +308,7 @@
         compiler_params=SMALL,
         name="prepare",
     )(*[pltpu.with_memory_space_constraint(a, pltpu.HBM) for a in raw])
-    records, crowded = across_two(first, second, crowded, chips, states)
+    records, crowded = across_two(own, pair, crowded, chips, states)
 
     state_shapes = (
         jax.ShapeDtypeStruct(state_mean.shape, state_mean.dtype),
@@ -334,8 +352,8 @@
         both = lax.all_gather(prior, "core")
         return jnp.sum(to_row(both[0] + both[1]), axis=0, dtype=BF16)
 
-    own = lax.cond(crowded[0] == 0, by_slot, whole, packed, prior, table)
-    sides = beside(own, chips, states)
+    prior_row = lax.cond(crowded[0] == 0, by_slot, whole, packed, prior, table)
+    sides = beside(prior_row, chips, states)
 
     return pl.pallas_call(
         second_kernel,
@@ -345,7 +363,7 @@
         scratch_shapes=[scaled],
         compiler_params=LARGE,
         name="second",
-    )(own, sides, errors, table, new_mean, new_anom, taper)
+    )(prior_row, sides, errors, table, new_mean, new_anom, taper)
 
 
 def solution(mesh):

time: 60.3 us -> 58.5 us (0.970)
  blocking collectives: 52.5 us -> 51.2 us
    all_to_all x1, blocking collectives: 13.8 us -> 12.4 us  [across_two(): lax.all_to_all(sent, ('state', 'chip', 'core'), 0, 0, axis_index_groups=g...]
    all_gather x1, blocking collectives: 8.68 us -> 9.79 us  [across_two(): return lax.optimization_barrier((lax.all_gather(dealt, 'core'), crowded))]
    all_to_all x1, blocking collectives: 11.1 us -> 10.1 us  [to_row(): lax.all_to_all(jnp.broadcast_to(part[None], (chips,) + part.shape), 'chip...]
where the time goes in v5:
time: 58.5 us; the launch traced here: 58.2 us
  blocking collectives  51.2 us (88%)
  Pallas kernels  6.13 us (10%)
  between operations  0.69 us (1%)
    all_to_all x1, blocking collectives, across_two(): lax.all_to_all(sent, ('state', 'chip', 'core'), 0, 0, axis_index_groups=g...  12.4 us
    all_to_all x1, blocking collectives, to_row(): lax.all_to_all(jnp.broadcast_to(part[None], (chips,) + part.shape), 'chip...  10.1 us
    all_gather x1, blocking collectives, across_two(): return lax.optimization_barrier((lax.all_gather(dealt, 'core'), crowded))  9.79 us
    all_gather x1, blocking collectives, across_two(): pair = lax.all_gather(pair, 'core')  8.37 us
    all_gather x1, blocking collectives, beside(): lax.all_gather(rows, ('state', 'chip', 'core'), axis_index_groups=groups)  4.84 us
    all_gather x1, blocking collectives, by_slot(): lax.all_gather(to_row(packed), 'core')  3.46 us
    pallas_call x1, Pallas kernels, local(): pl.pallas_call(first_kernel, out_shape=state_shapes + (jax.ShapeDtypeStru...  2.41 us
    all_gather x1, blocking collectives, beside(): return lax.all_gather(partner, 'core')  2.2 us

profile of v5, /device:TPU:1, one launch (start us, length us, event | category | flops | bytes accessed | tf_op | source)
XLA Modules:
  0.0 58.2 jit_solution(14309805065000578255)
XLA Ops:
  0.6 1.3 %prepare.1 = (bf16[48,128]{1,0:T(8,128)(2,1)S(1)}, bf16[48,128]{1,0:T(8,128)(2,1)S(1)}, s32[8,512]{1,0:T(8,128)S(1)}, f32[2,1024]{1,0:T(2,128)S(1)}, s32[1]{0:T(128)S(4)}) custom-call(bf16[2,32,80]{2,1,0:T(8,128)(2,1)} %bitcast.9, bf16[2,32]{1,0:T(2,128)(2,1)} %value_in.1, bf16[2,32]{1,0:T(2,128)(2,1)} %var_in.1, s32[1,512]{1,0:T(1,128)} %bitcast.10, ...), custom_call_target="tpu_custom_call" | custom-call | tf_op jit(solution)/shard_map/prepare/pallas_call | solution.py:296
  1.9 8.4 %all-gather.2 = bf16[96,128]{1,0:T(8,128)(2,1)S(1)} all-gather(bf16[48,128]{1,0:T(8,128)(2,1)S(1)} %get-tuple-element.25), channel_id=4, replica_groups=mesh['state'=32,'chip'=8,'core'=2] {'core'}, dimensions={0}, use_global_device_ids=true | all-gather | bytes 36864 | tf_op jit(solution)/shard_map/all_gather | solution.py:281
  10.3 0.1 broadcast_select_fusion
  10.4 0.0 copy-start.2
  10.4 12.4 %all_to_all.15 = bf16[16,48,128]{2,1,0:T(8,128)(2,1)S(1)} all-to-all(bf16[16,48,128]{2,1,0:T(8,128)(2,1)S(1)} %broadcast_select_fusion), channel_id=1, replica_groups={{1,3,5,7,9,11,13,15,16,18,20,22,24,26,28,30},{17,19,21,23,25,27,29,31,3..., dimensions={0} | all-to-all | bytes 393216 | tf_op jit(solution)/shard_map/all_to_all | solution.py:284
  22.8 0.0 copy-start
  22.8 0.0 copy-start.1
  22.8 9.8 %all-gather.3 = bf16[32,48,128]{2,1,0:T(8,128)(2,1)S(1)} all-gather(bf16[16,48,128]{2,1,0:T(8,128)(2,1)S(1)} %all_to_all.15), channel_id=5, replica_groups=mesh['state'=32,'chip'=8,'core'=2] {'core'}, dimensions={0}, use_global_device_ids=true | all-gather | bytes 589824 | tf_op jit(solution)/shard_map/all_gather | solution.py:285
  32.6 0.0 copy-done.2
  32.6 0.0 copy-done
  32.6 0.0 copy-done.1
  32.6 2.4 %first.1 = (f32[2,1024]{1,0:T(2,128)S(1)}, bf16[2,80,1024]{2,1,0:T(8,128)(2,1)S(1)}, bf16[40,128]{1,0:T(8,128)(2,1)S(1)}, bf16[80,512]{1,0:T(8,128)(2,1)S(1)}, bf16[16,1536]{1,0:T(8,128)(2,1)S(1)}) custom-call(bf16[2,16,48,128]{3,2,1,0:T(8,128)(2,1)S(1)} %bitcast.6, s32[8,512]{1,0:T(8,128)S(1)} %get-tuple-element.29.table_ref, f32[8,512]{1,0:T(8,128)S(1)} %copy-done.2, ...), custom_call_target="tpu_custom_call" | custom-call | tf_op jit(solution)/shard_map/first/pallas_call | solution.py:319
  35.0 14.0 %conditional.1 = (bf16[80,512]{1,0:T(8,128)(2,1)S(1)}) conditional(s32[]{:T(128)} %bitcast.4, bf16[80,512]{1,0:T(8,128)(2,1)S(1)} %get-tuple-element.31, (bf16[40,128]{1,0:T(8,128)(2,1)S(1)}, s32[8,512]{1,0:T(8,128)S(1)}) %tuple.15), branch_computations={%region_0.2_spmd, %region_2.3_spmd} | conditional | flops 327680 | bytes 3276810 | solution.py:355
  35.1 10.1 %all_to_all.14 = bf16[8,40,128]{2,1,0:T(8,128)(2,1)S(1)} all-to-all(bf16[8,40,128]{2,1,0:T(8,128)(2,1)S(1)} %broadcast_in_dim.32), channel_id=1, replica_groups=mesh['state'=32,'chip'=8,'core'=2] {'chip'}, dimensions={0} | all-to-all | bytes 163840 | tf_op jit(solution)/shard_map/cond/branch_1_fun/all_to_all | solution.py:339
  45.2 3.5 %all-gather.1 = bf16[16,40,128]{2,1,0:T(8,128)(2,1)S(1)} all-gather(bf16[8,40,128]{2,1,0:T(8,128)(2,1)S(1)} %all_to_all.14), channel_id=3, replica_groups=mesh['state'=32,'chip'=8,'core'=2] {'core'}, dimensions={0}, use_global_device_ids=true | all-gather | bytes 245760 | tf_op jit(solution)/shard_map/cond/branch_1_fun/all_gather | solution.py:349
  48.7 0.4 spread.1
  49.1 4.8 %all-gather.4 = bf16[160,512]{1,0:T(8,128)(2,1)S(1)} all-gather(bf16[80,512]{1,0:T(8,128)(2,1)S(1)} %get-tuple-element.36.own_ref), channel_id=6, replica_groups={{1,16},{3,18},{5,20},{7,22},{9,24},{11,26},{13,28},{15,30},{17,32},{19,..., dimensions={0}, use_global_device_ids=true | all-gather | bytes 245760 | tf_op jit(solution)/shard_map/all_gather | solution.py:271
  53.9 2.2 %all-gather.5 = bf16[160,512]{1,0:T(8,128)(2,1)S(1)} all-gather(bf16[80,512]{1,0:T(8,128)(2,1)S(1)} %slice_select_fusion), channel_id=7, replica_groups=mesh['state'=32,'chip'=8,'core'=2] {'core'}, dimensions={0}, use_global_device_ids=true | all-gather | bytes 245760 | tf_op jit(solution)/shard_map/all_gather | solution.py:273
  56.1 2.0 %second.1 = (f32[2,1024]{1,0:T(2,128)}, bf16[2,80,1024]{2,1,0:T(8,128)(2,1)}) custom-call(bf16[80,512]{1,0:T(8,128)(2,1)S(1)} %get-tuple-element.36.own_ref, bf16[2,80,512]{2,1,0:T(8,128)(2,1)S(1)} %bitcast.7, bf16[16,1536]{1,0:T(8,128)(2,1)S(1)} %get-tuple-element.33.errors_ref, s32[8,512]{1,0:T(8,128)S(1)} %get-tuple-element.29.table_ref, ...), custom_call_target="tpu_custom_call" | custom-call | tf_op jit(solution)/shard_map/second/pallas_call | solution.py:358
  (4 shorter events, 0.0 us)
Async XLA Ops:
  10.4 22.2 %copy-start.2 = (f32[8,512]{1,0:T(8,128)S(1)}, f32[8,512]{1,0:T(8,128)}, u32[]{:S(2)}) copy-start(f32[8,512]{1,0:T(8,128)} %weight_ref.1) | copy-start | bytes 49156
  22.8 9.8 %copy-start = (bf16[2,2,256,128]{3,2,1,0:T(8,128)(2,1)S(1)}, bf16[2,2,256,128]{3,2,1,0:T(8,128)(2,1)}, u32[]{:S(2)}) copy-start(bf16[2,2,256,128]{3,2,1,0:T(8,128)(2,1)} %taper_ref.3) | copy-start | bytes 786436
  22.8 9.8 %copy-start.1 = (bf16[2,80,1024]{2,1,0:T(8,128)(2,1)S(1)}, bf16[2,80,1024]{2,1,0:T(8,128)(2,1)}, u32[]{:S(2)}) copy-start(bf16[2,80,1024]{2,1,0:T(8,128)(2,1)} %anom_ref.1) | copy-start | bytes 983044

commit v6 on v5

--- a/solution.py
+++ b/solution.py
@@ -84,11 +84,18 @@
         new_anom_ref[tile, :, cells] = new_anom
         if change_ref is not None:
             rise = new_mean_ref[tile : tile + 1, cells] - mean_ref[tile : tile + 1, cells]
-            change = (new_anom.astype(F32) - old + rise).astype(BF16)
+            high = rise.astype(BF16).astype(F32)
+            middle = (rise - high).astype(BF16).astype(F32)
+            row = iota((16, step), 0)
+            rises = jnp.where(row == 0, high, jnp.where(row == 1, middle, jnp.where(row == 2, rise - high - middle, 0.0)))
+            stack = (new_anom, anom_ref[tile, :, cells], rises.astype(BF16))
             for part in range(2):
-                change_ref[start // width + part, :, tile * width : (tile + 1) * width] = change[
-                    :, part * width : (part + 1) * width
-                ]
+                at = 0
+                for values in stack:
+                    change_ref[start // width + part, at : at + values.shape[0], tile * width : (tile + 1) * width] = values[
+                        :, part * width : (part + 1) * width
+                    ]
+                    at += values.shape[0]
 
 
 def update_tiles(
@@ -128,8 +135,7 @@
     width = folded.shape[0] * 2 // 3
     beneath = folded[width:]
     other = jnp.concatenate([beneath, pltpu.roll(beneath, LANES // 2, 1)], axis=0)
-    lane = iota((width, LANES), 1)
-    return pltpu.roll(jnp.where(lane < KEPT, other, folded[:width]), LANES - KEPT, 1).astype(BF16)
+    return jnp.where(iota((width, LANES), 1) < KEPT, other, folded[:width]).astype(BF16)
 
 
 def prepare_kernel(
@@ -170,13 +176,17 @@
     device_columns = tiles * tile_columns
     own = own_chip * 2 + core
     column = home_ref[...] - state * (chips * 2 * device_columns)
-    device = jnp.zeros_like(column)
-    for edge in range(1, chips * 2):
-        device = device + jnp.where(column >= edge * device_columns, 1, 0)
-    device = device.astype(F32)
-    across = jnp.broadcast_to(device, (8, region)).T[:, 0:1]
-    earlier = (across == device) & (iota((region, region), 0) < iota((region, region), 1))
-    rank = jnp.sum(jnp.where(earlier, 1.0, 0.0), axis=0, keepdims=True)
+    first_column = iota((2 * chips, region), 0) * device_columns
+    at_home = (column >= first_column) & (column < first_column + device_columns)
+    at_home = jnp.where(at_home, 1.0, 0.0)
+    earlier = one_hot(iota((LANES, LANES), 0) < iota((LANES, LANES), 1))
+    ranks, before = [], jnp.zeros((2 * chips, 1), F32)
+    for start in range(0, region, LANES):
+        some = at_home[:, start : start + LANES]
+        ranks.append(jnp.sum(some * (dot(some.astype(BF16), earlier) + before), axis=0, keepdims=True))
+        before = before + jnp.sum(some, axis=1, keepdims=True)
+    rank = jnp.concatenate(ranks, axis=1)
+    device = jnp.sum(at_home * iota((2 * chips, region), 0).astype(F32), axis=0, keepdims=True)
     slot = (device * SLOTS + rank).astype(jnp.int32)
     table_ref[SLOT : SLOT + 1] = slot
     table_ref[MINE : MINE + 1] = slot - own * SLOTS
@@ -208,9 +218,22 @@
             here = at + core * width
             rows_ref[region + here : region + here + width] = folded[:width]
             rows_ref[3 * region + here : 3 * region + here + width] = unfold(folded)
-    turn = identity(LANES)
-    fields = dot(turn, rows_ref[...], ((1,), (1,)))
-    listed = fields[: members + 16, : 3 * region].astype(BF16)
+    count = members + 16
+    field, lane = iota((count, LANES), 0), iota((count, LANES), 1)
+    plain = one_hot(field == lane)
+    turned = one_hot(jnp.where(field < LANES - KEPT, field + KEPT, field + KEPT - LANES) == lane)
+    both = jnp.concatenate([plain, turned], axis=0)
+    on_first = jnp.bitwise_and(iota((count, region), 1), 2 * width - 1) < width
+    listed = []
+    for part in range(3):
+        rows = rows_ref[part * region : (part + 1) * region]
+        if part == 1:
+            listed.append(dot(plain, rows, ((1,), (1,))).astype(BF16))
+        else:
+            fields = dot(both, rows, ((1,), (1,)))
+            listed.append(jnp.where(on_first, fields[:count], fields[count:]).astype(BF16))
+    listed = jnp.concatenate(listed, axis=1)
+    prior = dot(turned[:members], rows_ref[3 * region :], ((1,), (1,)))
     errors_ref[...] = listed[members:]
     update_tiles(
         listed, table_ref, 0, members, members, mean_ref, anom_ref, taper_ref,
@@ -219,10 +242,12 @@
     home = table_ref[NEAR : NEAR + 1]
     columns = change_ref.shape[2]
     at_home = one_hot(iota((columns, region), 0) == home)
-    prior = fields[:members, 3 * region :]
     increment = None
     for level in range(change_ref.shape[0]):
-        part = dot(change_ref[level], at_home) * weight_ref[level : level + 1]
+        chosen = dot(change_ref[level], at_home)
+        rise = chosen[2 * members : 2 * members + 1] + chosen[2 * members + 1 : 2 * members + 2]
+        rise = rise + chosen[2 * members + 2 : 2 * members + 3]
+        part = (chosen[:members] - chosen[members : 2 * members] + rise) * weight_ref[level : level + 1]
         increment = part if increment is None else increment + part
     inside = (home >= 0) & (home < columns)
     updated = jnp.where(inside, prior + increment, 0.0).astype(BF16)
@@ -329,7 +354,7 @@
         scratch_shapes=[
             pltpu.VMEM((4 * region, LANES), BF16),
             scaled,
-            pltpu.VMEM((cells // tile_width, members, tiles * tile_width), BF16),
+            pltpu.VMEM((cells // tile_width, 2 * members + 16, tiles * tile_width), BF16),
         ],
         compiler_params=LARGE,
         name="first",

time: 58.5 us -> 58.4 us (level)
  no operation moved by 1% of the time
where the time goes in v6:
time: 58.4 us; the launch traced here: 58 us
  blocking collectives  51.2 us (88%)
  Pallas kernels  5.95 us (10%)
  between operations  0.69 us (1%)
    all_to_all x1, blocking collectives, across_two(): lax.all_to_all(sent, ('state', 'chip', 'core'), 0, 0, axis_index_groups=g...  12.4 us
    all_to_all x1, blocking collectives, to_row(): lax.all_to_all(jnp.broadcast_to(part[None], (chips,) + part.shape), 'chip...  10.1 us
    all_gather x1, blocking collectives, across_two(): return lax.optimization_barrier((lax.all_gather(dealt, 'core'), crowded))  9.79 us
    all_gather x1, blocking collectives, across_two(): pair = lax.all_gather(pair, 'core')  8.37 us
    all_gather x1, blocking collectives, beside(): lax.all_gather(rows, ('state', 'chip', 'core'), axis_index_groups=groups)  4.84 us
    all_gather x1, blocking collectives, by_slot(): lax.all_gather(to_row(packed), 'core')  3.46 us
    pallas_call x1, Pallas kernels, local(): pl.pallas_call(first_kernel, out_shape=state_shapes + (jax.ShapeDtypeStru...  2.31 us
    all_gather x1, blocking collectives, beside(): return lax.all_gather(partner, 'core')  2.2 us

profile of v6, /device:TPU:1, one launch (start us, length us, event | category | flops | bytes accessed | tf_op | source)
XLA Modules:
  0.0 58.0 jit_solution(3182237401192842223)
XLA Ops:
  0.6 1.2 %prepare.1 = (bf16[48,128]{1,0:T(8,128)(2,1)S(1)}, bf16[48,128]{1,0:T(8,128)(2,1)S(1)}, s32[8,512]{1,0:T(8,128)S(1)}, f32[2,1024]{1,0:T(2,128)S(1)}, s32[1]{0:T(128)S(4)}) custom-call(bf16[2,32,80]{2,1,0:T(8,128)(2,1)} %bitcast.9, bf16[2,32]{1,0:T(2,128)(2,1)} %value_in.1, bf16[2,32]{1,0:T(2,128)(2,1)} %var_in.1, s32[1,512]{1,0:T(1,128)} %bitcast.10, ...), custom_call_target="tpu_custom_call" | custom-call | tf_op jit(solution)/shard_map/prepare/pallas_call | solution.py:321
  1.8 8.4 %all-gather.2 = bf16[96,128]{1,0:T(8,128)(2,1)S(1)} all-gather(bf16[48,128]{1,0:T(8,128)(2,1)S(1)} %get-tuple-element.25), channel_id=4, replica_groups=mesh['state'=32,'chip'=8,'core'=2] {'core'}, dimensions={0}, use_global_device_ids=true | all-gather | bytes 36864 | tf_op jit(solution)/shard_map/all_gather | solution.py:306
  10.2 0.1 broadcast_select_fusion
  10.3 0.0 copy-start.2
  10.3 12.4 %all_to_all.15 = bf16[16,48,128]{2,1,0:T(8,128)(2,1)S(1)} all-to-all(bf16[16,48,128]{2,1,0:T(8,128)(2,1)S(1)} %broadcast_select_fusion), channel_id=1, replica_groups={{1,3,5,7,9,11,13,15,16,18,20,22,24,26,28,30},{17,19,21,23,25,27,29,31,3..., dimensions={0} | all-to-all | bytes 393216 | tf_op jit(solution)/shard_map/all_to_all | solution.py:309
  22.7 0.0 copy-start
  22.7 0.0 copy-start.1
  22.7 9.8 %all-gather.3 = bf16[32,48,128]{2,1,0:T(8,128)(2,1)S(1)} all-gather(bf16[16,48,128]{2,1,0:T(8,128)(2,1)S(1)} %all_to_all.15), channel_id=5, replica_groups=mesh['state'=32,'chip'=8,'core'=2] {'core'}, dimensions={0}, use_global_device_ids=true | all-gather | bytes 589824 | tf_op jit(solution)/shard_map/all_gather | solution.py:310
  32.5 0.0 copy-done.2
  32.5 0.0 copy-done
  32.5 0.0 copy-done.1
  32.5 2.3 %first.1 = (f32[2,1024]{1,0:T(2,128)S(1)}, bf16[2,80,1024]{2,1,0:T(8,128)(2,1)S(1)}, bf16[40,128]{1,0:T(8,128)(2,1)S(1)}, bf16[80,512]{1,0:T(8,128)(2,1)S(1)}, bf16[16,1536]{1,0:T(8,128)(2,1)S(1)}) custom-call(bf16[2,16,48,128]{3,2,1,0:T(8,128)(2,1)S(1)} %bitcast.6, s32[8,512]{1,0:T(8,128)S(1)} %get-tuple-element.29.table_ref, f32[8,512]{1,0:T(8,128)S(1)} %copy-done.2, ...), custom_call_target="tpu_custom_call" | custom-call | tf_op jit(solution)/shard_map/first/pallas_call | solution.py:344
  34.9 14.0 %conditional.1 = (bf16[80,512]{1,0:T(8,128)(2,1)S(1)}) conditional(s32[]{:T(128)} %bitcast.4, bf16[80,512]{1,0:T(8,128)(2,1)S(1)} %get-tuple-element.31, (bf16[40,128]{1,0:T(8,128)(2,1)S(1)}, s32[8,512]{1,0:T(8,128)S(1)}) %tuple.15), branch_computations={%region_0.2_spmd, %region_2.3_spmd} | conditional | flops 327680 | bytes 3276810 | solution.py:380
  34.9 10.1 %all_to_all.14 = bf16[8,40,128]{2,1,0:T(8,128)(2,1)S(1)} all-to-all(bf16[8,40,128]{2,1,0:T(8,128)(2,1)S(1)} %broadcast_in_dim.32), channel_id=1, replica_groups=mesh['state'=32,'chip'=8,'core'=2] {'chip'}, dimensions={0} | all-to-all | bytes 163840 | tf_op jit(solution)/shard_map/cond/branch_1_fun/all_to_all | solution.py:364
  45.0 3.5 %all-gather.1 = bf16[16,40,128]{2,1,0:T(8,128)(2,1)S(1)} all-gather(bf16[8,40,128]{2,1,0:T(8,128)(2,1)S(1)} %all_to_all.14), channel_id=3, replica_groups=mesh['state'=32,'chip'=8,'core'=2] {'core'}, dimensions={0}, use_global_device_ids=true | all-gather | bytes 245760 | tf_op jit(solution)/shard_map/cond/branch_1_fun/all_gather | solution.py:374
  48.5 0.4 spread.1
  48.9 4.8 %all-gather.4 = bf16[160,512]{1,0:T(8,128)(2,1)S(1)} all-gather(bf16[80,512]{1,0:T(8,128)(2,1)S(1)} %get-tuple-element.36.own_ref), channel_id=6, replica_groups={{1,16},{3,18},{5,20},{7,22},{9,24},{11,26},{13,28},{15,30},{17,32},{19,..., dimensions={0}, use_global_device_ids=true | all-gather | bytes 245760 | tf_op jit(solution)/shard_map/all_gather | solution.py:296
  53.7 2.2 %all-gather.5 = bf16[160,512]{1,0:T(8,128)(2,1)S(1)} all-gather(bf16[80,512]{1,0:T(8,128)(2,1)S(1)} %slice_select_fusion), channel_id=7, replica_groups=mesh['state'=32,'chip'=8,'core'=2] {'core'}, dimensions={0}, use_global_device_ids=true | all-gather | bytes 245760 | tf_op jit(solution)/shard_map/all_gather | solution.py:298
  55.9 2.1 %second.1 = (f32[2,1024]{1,0:T(2,128)}, bf16[2,80,1024]{2,1,0:T(8,128)(2,1)}) custom-call(bf16[80,512]{1,0:T(8,128)(2,1)S(1)} %get-tuple-element.36.own_ref, bf16[2,80,512]{2,1,0:T(8,128)(2,1)S(1)} %bitcast.7, bf16[16,1536]{1,0:T(8,128)(2,1)S(1)} %get-tuple-element.33.errors_ref, s32[8,512]{1,0:T(8,128)S(1)} %get-tuple-element.29.table_ref, ...), custom_call_target="tpu_custom_call" | custom-call | tf_op jit(solution)/shard_map/second/pallas_call | solution.py:383
  (4 shorter events, 0.0 us)
Async XLA Ops:
  10.3 22.2 %copy-start.2 = (f32[8,512]{1,0:T(8,128)S(1)}, f32[8,512]{1,0:T(8,128)}, u32[]{:S(2)}) copy-start(f32[8,512]{1,0:T(8,128)} %weight_ref.1) | copy-start | bytes 49156
  22.7 9.8 %copy-start = (bf16[2,2,256,128]{3,2,1,0:T(8,128)(2,1)S(1)}, bf16[2,2,256,128]{3,2,1,0:T(8,128)(2,1)}, u32[]{:S(2)}) copy-start(bf16[2,2,256,128]{3,2,1,0:T(8,128)(2,1)} %taper_ref.3) | copy-start | bytes 786436
  22.7 9.8 %copy-start.1 = (bf16[2,80,1024]{2,1,0:T(8,128)(2,1)S(1)}, bf16[2,80,1024]{2,1,0:T(8,128)(2,1)}, u32[]{:S(2)}) copy-start(bf16[2,80,1024]{2,1,0:T(8,128)(2,1)} %anom_ref.1) | copy-start | bytes 983044

commit v7 on v6

--- a/solution.py
+++ b/solution.py
@@ -1,5 +1,3 @@
-import functools
-
 import jax
 import jax.numpy as jnp
 from jax import lax
@@ -139,8 +137,8 @@
 
 
 def prepare_kernel(
-    chips, tile_columns, prior_in, value_in, var_in, home_in, lists_in, mean_in,
-    own_ref, pair_ref, table_ref, mean_ref, crowded_ref, prior_ref, value_ref, var_ref, home_ref, lists_ref, sems,
+    prior_in, value_in, var_in, home_in, lists_in, mean_in,
+    own_ref, pair_ref, home_ref, lists_ref, mean_ref, prior_ref, value_ref, var_ref, sems,
 ):
     copies = [
         pltpu.make_async_copy(source, target, sems.at[i])
@@ -170,6 +168,9 @@
     on_first = lax.axis_index("core") == 0
     own_ref[...] = fold(first, second)
     pair_ref[...] = fold(jnp.where(on_first, first, none), jnp.where(on_first, none, first))
+
+
+def plan(chips, tile_columns, home_ref, lists_ref, table_ref, crowded_ref):
     colours, tiles, length = lists_ref.shape
     region = home_ref.shape[1]
     state, own_chip, core = lax.axis_index("state"), lax.axis_index("chip"), lax.axis_index("core")
@@ -200,13 +201,14 @@
 
 
 def first_kernel(
-    records_ref, table_ref, weight_ref, mean_ref, anom_ref, taper_ref,
-    new_mean_ref, new_anom_ref, packed_ref, prior_ref, errors_ref, rows_ref, scaled_ref, change_ref,
+    records_ref, home_ref, lists_ref, weight_ref, mean_ref, anom_ref, taper_ref,
+    new_mean_ref, new_anom_ref, packed_ref, prior_ref, errors_ref, table_ref, crowded_ref, rows_ref, scaled_ref, change_ref,
 ):
     members = anom_ref.shape[1]
     _, dealt, height, _ = records_ref.shape
     chips, width = dealt // 2, height * 2 // 3
     region = 2 * chips * width
+    plan(chips, taper_ref.shape[3], home_ref, lists_ref, table_ref, crowded_ref)
     for chip in range(chips):
         at = chip * 2 * width
         for side, part in ((0, 0), (1, 2)):
@@ -298,7 +300,7 @@
     return lax.all_gather(partner, "core")
 
 
-def across_two(own, pair, crowded, chips, states):
+def across_two(own, pair, chips, states):
     at = lambda state, chip, core: (state * chips + chip) * 2 + core
     groups = [
         [at(s, c, 1) for c in range(chips)] + [at((s + 1) % states, c, 0) for c in range(chips)] for s in range(states)
@@ -307,7 +309,7 @@
     low = (lax.iota(jnp.int32, 2 * chips) < chips) == (lax.axis_index("core") == 1)
     sent = jnp.where(low[:, None, None], own[None], (pair[0] + pair[1])[None])
     dealt = lax.all_to_all(sent, ("state", "chip", "core"), 0, 0, axis_index_groups=groups)
-    return lax.optimization_barrier((lax.all_gather(dealt, "core"), crowded))
+    return lax.all_gather(dealt, "core")
 
 
 def local(state_mean, state_anom, obs_prior, obs_value, obs_var, obs_weight, obs_home, tile_obs, taper):
@@ -318,22 +320,20 @@
     region = 2 * chips * width
     raw = (jnp.swapaxes(obs_prior, 1, 2), obs_value, obs_var, obs_home[None], tile_obs, state_mean)
     block = jax.ShapeDtypeStruct((width * 3 // 2, LANES), BF16)
-    own, pair, table, mean, crowded = pl.pallas_call(
-        functools.partial(prepare_kernel, chips, tile_width),
+    own, pair, home, lists, mean = pl.pallas_call(
+        prepare_kernel,
         out_shape=(
             block,
             block,
-            jax.ShapeDtypeStruct((8, region), jnp.int32),
-            jax.ShapeDtypeStruct(state_mean.shape, state_mean.dtype),
-            pltpu.SMEM((1,), jnp.int32),
+            *(jax.ShapeDtypeStruct(a.shape, a.dtype) for a in raw[3:]),
         ),
         in_specs=[pl.BlockSpec(memory_space=pltpu.HBM)] * len(raw),
-        out_specs=(VMEM, VMEM, VMEM, VMEM, SMEM),
-        scratch_shapes=[pltpu.VMEM(a.shape, a.dtype) for a in raw[:-1]] + [pltpu.SemaphoreType.DMA((len(raw),))],
+        out_specs=(VMEM,) * 5,
+        scratch_shapes=[pltpu.VMEM(a.shape, a.dtype) for a in raw[:3]] + [pltpu.SemaphoreType.DMA((len(raw),))],
         compiler_params=SMALL,
         name="prepare",
     )(*[pltpu.with_memory_space_constraint(a, pltpu.HBM) for a in raw])
-    records, crowded = across_two(own, pair, crowded, chips, states)
+    records = across_two(own, pair, chips, states)
 
     state_shapes = (
         jax.ShapeDtypeStruct(state_mean.shape, state_mean.dtype),
@@ -341,16 +341,18 @@
     )
     scaled = pltpu.VMEM((tiles, tile_obs.shape[2], cells), BF16)
     prior_shape = jax.ShapeDtypeStruct((members, region), BF16)
-    new_mean, new_anom, packed, prior, errors = pl.pallas_call(
+    new_mean, new_anom, packed, prior, errors, table, crowded = pl.pallas_call(
         first_kernel,
         out_shape=state_shapes
         + (
             jax.ShapeDtypeStruct((members // 2, LANES), BF16),
             prior_shape,
             jax.ShapeDtypeStruct((16, 3 * region), BF16),
+            jax.ShapeDtypeStruct((8, region), jnp.int32),
+            pltpu.SMEM((1,), jnp.int32),
         ),
-        in_specs=[VMEM] * 6,
-        out_specs=(VMEM,) * 5,
+        in_specs=[VMEM] * 7,
+        out_specs=(VMEM,) * 6 + (SMEM,),
         scratch_shapes=[
             pltpu.VMEM((4 * region, LANES), BF16),
             scaled,
@@ -358,7 +360,7 @@
         ],
         compiler_params=LARGE,
         name="first",
-    )(records, table, obs_weight, mean, state_anom, taper)
+    )(records, home, lists, obs_weight, mean, state_anom, taper)
 
     def to_row(part):
         return lax.all_to_all(jnp.broadcast_to(part[None], (chips,) + part.shape), "chip", 0, 0)

time: 58.4 us -> 58.4 us (level)
  no operation moved by 1% of the time
where the time goes in v7:
time: 58.4 us; the launch traced here: 58 us
  blocking collectives  51.2 us (88%)
  Pallas kernels  5.98 us (10%)
  between operations  0.69 us (1%)
    all_to_all x1, blocking collectives, across_two(): lax.all_to_all(sent, ('state', 'chip', 'core'), 0, 0, axis_index_groups=g...  12.4 us
    all_to_all x1, blocking collectives, to_row(): lax.all_to_all(jnp.broadcast_to(part[None], (chips,) + part.shape), 'chip...  10.1 us
    all_gather x1, blocking collectives, across_two(): return lax.all_gather(dealt, 'core')  9.79 us
    all_gather x1, blocking collectives, across_two(): pair = lax.all_gather(pair, 'core')  8.37 us
    all_gather x1, blocking collectives, beside(): lax.all_gather(rows, ('state', 'chip', 'core'), axis_index_groups=groups)  4.84 us
    all_gather x1, blocking collectives, by_slot(): lax.all_gather(to_row(packed), 'core')  3.45 us
    pallas_call x1, Pallas kernels, local(): pl.pallas_call(first_kernel, out_shape=state_shapes + (jax.ShapeDtypeStru...  2.38 us
    all_gather x1, blocking collectives, beside(): return lax.all_gather(partner, 'core')  2.21 us

profile of v7, /device:TPU:1, one launch (start us, length us, event | category | flops | bytes accessed | tf_op | source)
XLA Modules:
  0.0 58.0 jit_solution(4213349447509159266)
XLA Ops:
  0.6 1.1 %prepare.1 = (bf16[48,128]{1,0:T(8,128)(2,1)S(1)}, bf16[48,128]{1,0:T(8,128)(2,1)S(1)}, s32[1,512]{1,0:T(1,128)S(1)}, s32[2,2,256]{2,1,0:T(2,128)S(1)}, f32[2,1024]{1,0:T(2,128)S(1)}) custom-call(bf16[2,32,80]{2,1,0:T(8,128)(2,1)} %bitcast.9, bf16[2,32]{1,0:T(2,128)(2,1)} %value_in.1, bf16[2,32]{1,0:T(2,128)(2,1)} %var_in.1, s32[1,512]{1,0:T(1,128)} %bitcast.10, ...), custom_call_target="tpu_custom_call" | custom-call | tf_op jit(solution)/shard_map/prepare/pallas_call | solution.py:323
  1.8 8.4 %all-gather.2 = bf16[96,128]{1,0:T(8,128)(2,1)S(1)} all-gather(bf16[48,128]{1,0:T(8,128)(2,1)S(1)} %get-tuple-element.25), channel_id=4, replica_groups=mesh['state'=32,'chip'=8,'core'=2] {'core'}, dimensions={0}, use_global_device_ids=true | all-gather | bytes 36864 | tf_op jit(solution)/shard_map/all_gather | solution.py:308
  10.1 0.1 broadcast_select_fusion
  10.2 0.0 copy-start.2
  10.3 12.4 %all_to_all.15 = bf16[16,48,128]{2,1,0:T(8,128)(2,1)S(1)} all-to-all(bf16[16,48,128]{2,1,0:T(8,128)(2,1)S(1)} %broadcast_select_fusion), channel_id=1, replica_groups={{1,3,5,7,9,11,13,15,16,18,20,22,24,26,28,30},{17,19,21,23,25,27,29,31,3..., dimensions={0} | all-to-all | bytes 393216 | tf_op jit(solution)/shard_map/all_to_all | solution.py:311
  22.7 0.0 copy-start
  22.7 0.0 copy-start.1
  22.7 9.8 %all-gather.3 = bf16[32,48,128]{2,1,0:T(8,128)(2,1)S(1)} all-gather(bf16[16,48,128]{2,1,0:T(8,128)(2,1)S(1)} %all_to_all.15), channel_id=5, replica_groups=mesh['state'=32,'chip'=8,'core'=2] {'core'}, dimensions={0}, use_global_device_ids=true | all-gather | bytes 589824 | tf_op jit(solution)/shard_map/all_gather | solution.py:312
  32.5 0.0 copy-done.2
  32.5 0.0 copy-done
  32.5 0.0 copy-done.1
  32.5 2.4 %first.1 = (f32[2,1024]{1,0:T(2,128)S(1)}, bf16[2,80,1024]{2,1,0:T(8,128)(2,1)S(1)}, bf16[40,128]{1,0:T(8,128)(2,1)S(1)}, bf16[80,512]{1,0:T(8,128)(2,1)S(1)}, b...) custom-call(bf16[2,16,48,128]{3,2,1,0:T(8,128)(2,1)S(1)} %bitcast.6, ...), custom_call_target="tpu_custom_call" | custom-call | tf_op jit(solution)/shard_map/first/pallas_call | solution.py:344
  34.9 14.0 %conditional.1 = (bf16[80,512]{1,0:T(8,128)(2,1)S(1)}) conditional(s32[]{:T(128)} %bitcast.4, bf16[80,512]{1,0:T(8,128)(2,1)S(1)} %get-tuple-element.30, (bf16[40,128]{1,0:T(8,128)(2,1)S(1)}, s32[8,512]{1,0:T(8,128)S(1)}) %tuple.13), branch_computations={%region_0.2_spmd, %region_2.3_spmd} | conditional | flops 327680 | bytes 3276810 | solution.py:382
  34.9 10.1 %all_to_all.14 = bf16[8,40,128]{2,1,0:T(8,128)(2,1)S(1)} all-to-all(bf16[8,40,128]{2,1,0:T(8,128)(2,1)S(1)} %broadcast_in_dim.32), channel_id=1, replica_groups=mesh['state'=32,'chip'=8,'core'=2] {'chip'}, dimensions={0} | all-to-all | bytes 163840 | tf_op jit(solution)/shard_map/cond/branch_1_fun/all_to_all | solution.py:366
  45.0 3.5 %all-gather.1 = bf16[16,40,128]{2,1,0:T(8,128)(2,1)S(1)} all-gather(bf16[8,40,128]{2,1,0:T(8,128)(2,1)S(1)} %all_to_all.14), channel_id=3, replica_groups=mesh['state'=32,'chip'=8,'core'=2] {'core'}, dimensions={0}, use_global_device_ids=true | all-gather | bytes 245760 | tf_op jit(solution)/shard_map/cond/branch_1_fun/all_gather | solution.py:376
  48.5 0.4 spread.1
  48.9 4.8 %all-gather.4 = bf16[160,512]{1,0:T(8,128)(2,1)S(1)} all-gather(bf16[80,512]{1,0:T(8,128)(2,1)S(1)} %get-tuple-element.36.own_ref), channel_id=6, replica_groups={{1,16},{3,18},{5,20},{7,22},{9,24},{11,26},{13,28},{15,30},{17,32},{19,..., dimensions={0}, use_global_device_ids=true | all-gather | bytes 245760 | tf_op jit(solution)/shard_map/all_gather | solution.py:298
  53.7 2.2 %all-gather.5 = bf16[160,512]{1,0:T(8,128)(2,1)S(1)} all-gather(bf16[80,512]{1,0:T(8,128)(2,1)S(1)} %slice_select_fusion), channel_id=7, replica_groups=mesh['state'=32,'chip'=8,'core'=2] {'core'}, dimensions={0}, use_global_device_ids=true | all-gather | bytes 245760 | tf_op jit(solution)/shard_map/all_gather | solution.py:300
  56.0 2.1 %second.1 = (f32[2,1024]{1,0:T(2,128)}, bf16[2,80,1024]{2,1,0:T(8,128)(2,1)}) custom-call(bf16[80,512]{1,0:T(8,128)(2,1)S(1)} %get-tuple-element.36.own_ref, bf16[2,80,512]{2,1,0:T(8,128)(2,1)S(1)} %bitcast.7, bf16[16,1536]{1,0:T(8,128)(2,1)S(1)} %get-tuple-element.33.errors_ref, s32[8,512]{1,0:T(8,128)S(1)} %get-tuple-element.32.table_ref, ...), custom_call_target="tpu_custom_call" | custom-call | tf_op jit(solution)/shard_map/second/pallas_call | solution.py:385
  (4 shorter events, 0.0 us)
Async XLA Ops:
  10.2 22.2 %copy-start.2 = (f32[8,512]{1,0:T(8,128)S(1)}, f32[8,512]{1,0:T(8,128)}, u32[]{:S(2)}) copy-start(f32[8,512]{1,0:T(8,128)} %weight_ref.1) | copy-start | bytes 49156
  22.7 9.8 %copy-start = (bf16[2,2,256,128]{3,2,1,0:T(8,128)(2,1)S(1)}, bf16[2,2,256,128]{3,2,1,0:T(8,128)(2,1)}, u32[]{:S(2)}) copy-start(bf16[2,2,256,128]{3,2,1,0:T(8,128)(2,1)} %taper_ref.3) | copy-start | bytes 786436
  22.7 9.8 %copy-start.1 = (bf16[2,80,1024]{2,1,0:T(8,128)(2,1)S(1)}, bf16[2,80,1024]{2,1,0:T(8,128)(2,1)}, u32[]{:S(2)}) copy-start(bf16[2,80,1024]{2,1,0:T(8,128)(2,1)} %anom_ref.1) | copy-start | bytes 983044

commit v8 on v6

--- a/solution.py
+++ b/solution.py
@@ -204,8 +204,8 @@
     new_mean_ref, new_anom_ref, packed_ref, prior_ref, errors_ref, rows_ref, scaled_ref, change_ref,
 ):
     members = anom_ref.shape[1]
-    _, dealt, height, _ = records_ref.shape
-    chips, width = dealt // 2, height * 2 // 3
+    _, dealt, folded_rows, _ = records_ref.shape
+    chips, width = dealt // 2, folded_rows * 2 // 3
     region = 2 * chips * width
     for chip in range(chips):
         at = chip * 2 * width
@@ -243,12 +243,17 @@
     columns = change_ref.shape[2]
     at_home = one_hot(iota((columns, region), 0) == home)
     increment = None
-    for level in range(change_ref.shape[0]):
-        chosen = dot(change_ref[level], at_home)
-        rise = chosen[2 * members : 2 * members + 1] + chosen[2 * members + 1 : 2 * members + 2]
-        rise = rise + chosen[2 * members + 2 : 2 * members + 3]
-        part = (chosen[:members] - chosen[members : 2 * members] + rise) * weight_ref[level : level + 1]
-        increment = part if increment is None else increment + part
+    levels, height, _ = change_ref.shape
+    together = 4
+    for start in range(0, levels, together):
+        several = change_ref[start : start + together].reshape(together * height, columns)
+        several = dot(several, at_home)
+        for level in range(start, start + together):
+            chosen = several[(level - start) * height : (level - start + 1) * height]
+            rise = chosen[2 * members : 2 * members + 1] + chosen[2 * members + 1 : 2 * members + 2]
+            rise = rise + chosen[2 * members + 2 : 2 * members + 3]
+            part = (chosen[:members] - chosen[members : 2 * members] + rise) * weight_ref[level : level + 1]
+            increment = part if increment is None else increment + part
     inside = (home >= 0) & (home < columns)
     updated = jnp.where(inside, prior + increment, 0.0).astype(BF16)
     prior_ref[...] = updated

time: 58.4 us -> 58.3 us (level)
  no operation moved by 1% of the time
where the time goes in v8:
time: 58.3 us; the launch traced here: 58 us
  blocking collectives  51.2 us (88%)
  Pallas kernels  5.95 us (10%)
  between operations  0.69 us (1%)
    all_to_all x1, blocking collectives, across_two(): lax.all_to_all(sent, ('state', 'chip', 'core'), 0, 0, axis_index_groups=g...  12.4 us
    all_to_all x1, blocking collectives, to_row(): lax.all_to_all(jnp.broadcast_to(part[None], (chips,) + part.shape), 'chip...  10.1 us
    all_gather x1, blocking collectives, across_two(): return lax.optimization_barrier((lax.all_gather(dealt, 'core'), crowded))  9.79 us
    all_gather x1, blocking collectives, across_two(): pair = lax.all_gather(pair, 'core')  8.37 us
    all_gather x1, blocking collectives, beside(): lax.all_gather(rows, ('state', 'chip', 'core'), axis_index_groups=groups)  4.84 us
    all_gather x1, blocking collectives, by_slot(): lax.all_gather(to_row(packed), 'core')  3.46 us
    pallas_call x1, Pallas kernels, local(): pl.pallas_call(first_kernel, out_shape=state_shapes + (jax.ShapeDtypeStru...  2.31 us
    all_gather x1, blocking collectives, beside(): return lax.all_gather(partner, 'core')  2.21 us

profile of v8, /device:TPU:1, one launch (start us, length us, event | category | flops | bytes accessed | tf_op | source)
XLA Modules:
  0.0 58.0 jit_solution(6163177329369604627)
XLA Ops:
  0.6 1.2 %prepare.1 = (bf16[48,128]{1,0:T(8,128)(2,1)S(1)}, bf16[48,128]{1,0:T(8,128)(2,1)S(1)}, s32[8,512]{1,0:T(8,128)S(1)}, f32[2,1024]{1,0:T(2,128)S(1)}, s32[1]{0:T(128)S(4)}) custom-call(bf16[2,32,80]{2,1,0:T(8,128)(2,1)} %bitcast.9, bf16[2,32]{1,0:T(2,128)(2,1)} %value_in.1, bf16[2,32]{1,0:T(2,128)(2,1)} %var_in.1, s32[1,512]{1,0:T(1,128)} %bitcast.10, ...), custom_call_target="tpu_custom_call" | custom-call | tf_op jit(solution)/shard_map/prepare/pallas_call | solution.py:326
  1.8 8.4 %all-gather.2 = bf16[96,128]{1,0:T(8,128)(2,1)S(1)} all-gather(bf16[48,128]{1,0:T(8,128)(2,1)S(1)} %get-tuple-element.25), channel_id=4, replica_groups=mesh['state'=32,'chip'=8,'core'=2] {'core'}, dimensions={0}, use_global_device_ids=true | all-gather | bytes 36864 | tf_op jit(solution)/shard_map/all_gather | solution.py:311
  10.2 0.1 broadcast_select_fusion
  10.3 0.0 copy-start.2
  10.3 12.4 %all_to_all.15 = bf16[16,48,128]{2,1,0:T(8,128)(2,1)S(1)} all-to-all(bf16[16,48,128]{2,1,0:T(8,128)(2,1)S(1)} %broadcast_select_fusion), channel_id=1, replica_groups={{1,3,5,7,9,11,13,15,16,18,20,22,24,26,28,30},{17,19,21,23,25,27,29,31,3..., dimensions={0} | all-to-all | bytes 393216 | tf_op jit(solution)/shard_map/all_to_all | solution.py:314
  22.7 0.0 copy-start
  22.7 0.0 copy-start.1
  22.7 9.8 %all-gather.3 = bf16[32,48,128]{2,1,0:T(8,128)(2,1)S(1)} all-gather(bf16[16,48,128]{2,1,0:T(8,128)(2,1)S(1)} %all_to_all.15), channel_id=5, replica_groups=mesh['state'=32,'chip'=8,'core'=2] {'core'}, dimensions={0}, use_global_device_ids=true | all-gather | bytes 589824 | tf_op jit(solution)/shard_map/all_gather | solution.py:315
  32.5 0.0 copy-done.2
  32.5 0.0 copy-done
  32.5 0.0 copy-done.1
  32.5 2.3 %first.1 = (f32[2,1024]{1,0:T(2,128)S(1)}, bf16[2,80,1024]{2,1,0:T(8,128)(2,1)S(1)}, bf16[40,128]{1,0:T(8,128)(2,1)S(1)}, bf16[80,512]{1,0:T(8,128)(2,1)S(1)}, bf16[16,1536]{1,0:T(8,128)(2,1)S(1)}) custom-call(bf16[2,16,48,128]{3,2,1,0:T(8,128)(2,1)S(1)} %bitcast.6, s32[8,512]{1,0:T(8,128)S(1)} %get-tuple-element.29.table_ref, f32[8,512]{1,0:T(8,128)S(1)} %copy-done.2, ...), custom_call_target="tpu_custom_call" | custom-call | tf_op jit(solution)/shard_map/first/pallas_call | solution.py:349
  34.9 14.0 %conditional.1 = (bf16[80,512]{1,0:T(8,128)(2,1)S(1)}) conditional(s32[]{:T(128)} %bitcast.4, bf16[80,512]{1,0:T(8,128)(2,1)S(1)} %get-tuple-element.31, (bf16[40,128]{1,0:T(8,128)(2,1)S(1)}, s32[8,512]{1,0:T(8,128)S(1)}) %tuple.15), branch_computations={%region_0.2_spmd, %region_2.3_spmd} | conditional | flops 327680 | bytes 3276810 | solution.py:385
  34.9 10.1 %all_to_all.14 = bf16[8,40,128]{2,1,0:T(8,128)(2,1)S(1)} all-to-all(bf16[8,40,128]{2,1,0:T(8,128)(2,1)S(1)} %broadcast_in_dim.32), channel_id=1, replica_groups=mesh['state'=32,'chip'=8,'core'=2] {'chip'}, dimensions={0} | all-to-all | bytes 163840 | tf_op jit(solution)/shard_map/cond/branch_1_fun/all_to_all | solution.py:369
  45.0 3.5 %all-gather.1 = bf16[16,40,128]{2,1,0:T(8,128)(2,1)S(1)} all-gather(bf16[8,40,128]{2,1,0:T(8,128)(2,1)S(1)} %all_to_all.14), channel_id=3, replica_groups=mesh['state'=32,'chip'=8,'core'=2] {'core'}, dimensions={0}, use_global_device_ids=true | all-gather | bytes 245760 | tf_op jit(solution)/shard_map/cond/branch_1_fun/all_gather | solution.py:379
  48.5 0.4 spread.1
  48.9 4.8 %all-gather.4 = bf16[160,512]{1,0:T(8,128)(2,1)S(1)} all-gather(bf16[80,512]{1,0:T(8,128)(2,1)S(1)} %get-tuple-element.36.own_ref), channel_id=6, replica_groups={{1,16},{3,18},{5,20},{7,22},{9,24},{11,26},{13,28},{15,30},{17,32},{19,..., dimensions={0}, use_global_device_ids=true | all-gather | bytes 245760 | tf_op jit(solution)/shard_map/all_gather | solution.py:301
  53.7 2.2 %all-gather.5 = bf16[160,512]{1,0:T(8,128)(2,1)S(1)} all-gather(bf16[80,512]{1,0:T(8,128)(2,1)S(1)} %slice_select_fusion), channel_id=7, replica_groups=mesh['state'=32,'chip'=8,'core'=2] {'core'}, dimensions={0}, use_global_device_ids=true | all-gather | bytes 245760 | tf_op jit(solution)/shard_map/all_gather | solution.py:303
  55.9 2.1 %second.1 = (f32[2,1024]{1,0:T(2,128)}, bf16[2,80,1024]{2,1,0:T(8,128)(2,1)}) custom-call(bf16[80,512]{1,0:T(8,128)(2,1)S(1)} %get-tuple-element.36.own_ref, bf16[2,80,512]{2,1,0:T(8,128)(2,1)S(1)} %bitcast.7, bf16[16,1536]{1,0:T(8,128)(2,1)S(1)} %get-tuple-element.33.errors_ref, s32[8,512]{1,0:T(8,128)S(1)} %get-tuple-element.29.table_ref, ...), custom_call_target="tpu_custom_call" | custom-call | tf_op jit(solution)/shard_map/second/pallas_call | solution.py:388
  (4 shorter events, 0.0 us)
Async XLA Ops:
  10.3 22.2 %copy-start.2 = (f32[8,512]{1,0:T(8,128)S(1)}, f32[8,512]{1,0:T(8,128)}, u32[]{:S(2)}) copy-start(f32[8,512]{1,0:T(8,128)} %weight_ref.1) | copy-start | bytes 49156
  22.7 9.8 %copy-start = (bf16[2,2,256,128]{3,2,1,0:T(8,128)(2,1)S(1)}, bf16[2,2,256,128]{3,2,1,0:T(8,128)(2,1)}, u32[]{:S(2)}) copy-start(bf16[2,2,256,128]{3,2,1,0:T(8,128)(2,1)} %taper_ref.3) | copy-start | bytes 786436
  22.7 9.8 %copy-start.1 = (bf16[2,80,1024]{2,1,0:T(8,128)(2,1)S(1)}, bf16[2,80,1024]{2,1,0:T(8,128)(2,1)}, u32[]{:S(2)}) copy-start(bf16[2,80,1024]{2,1,0:T(8,128)(2,1)} %anom_ref.1) | copy-start | bytes 983044
